TPU v7x, 512 devices: a whole 4x8x8 slice. The times are simulated.
512 devices in a mesh: row: 16 (over y, x_lo), col: 32 (over x_hi, z, core).
Axes of the slice: x: 4 (x_hi: 2, x_lo: 2; x = x_hi * 2 + x_lo), y: 8, z: 8, core: 2. Of those that a mesh axis runs over, the one named last changes fastest.
Arguments:
- tokens: bfloat16 [65536, 3584], P(('row', 'col')), may hold values from -6 to 6
- targets: bfloat16 [65536, 3584], P(('row', 'col')), may hold values from -6 to 6
- w_up: bfloat16 [32, 3584, 448], P('col', 'row'), may hold values from -6 to 6
- w_down: bfloat16 [16, 3584, 448], P('row', 'col'), may hold values from -6 to 6
- up_momentum: float32 [32, 3584, 448], P('col', 'row'), may hold values from -2 to 2
- down_momentum: float32 [16, 3584, 448], P('row', 'col'), may hold values from -2 to 2
- member_up: int32 [16, 32], replicated, may hold values from 0 to 1, as said below
- member_down: int32 [16, 32], replicated, may hold values from 0 to 1, as said below
- path_rate: float32 [16, 32], replicated, may hold values from 0.1 to 1
Outputs:
- new_up: bfloat16 [32, 3584, 448], P('col', 'row')
- new_up_momentum: float32 [32, 3584, 448], P('col', 'row')
- new_down: bfloat16 [16, 3584, 448], P('row', 'col')
- new_down_momentum: float32 [16, 3584, 448], P('row', 'col')
Inputs may be any that keep to these rules, and one draw needn't show every extreme that they name: Every column of member_up holds at least one 1. Every row of member_down holds at least one 1.
All inputs are finite; a program needn't handle non-finite values. Where the computation divides by a largest or mean magnitude, that divisor is 1e-20 or more.
Results may differ from a plain program's by a relative error of at most 0.006.
Values may be sent and summed in bfloat16 or wider, within the bound.
A program may use at most 64 MiB of HBM per device.

v0:
```python
import jax
import jax.numpy as jnp
from jax import lax
from jax.sharding import Mesh
from jax.sharding import PartitionSpec as P

ROW = ("row_0", "row_1")
ROW_COL = ("row_0", "row_1", "col")


def gathered_by_axis(x, axes, dim):
    filled = x
    for number in range(len(axes) - 1, -1, -1):
        filled = lax.all_gather(filled, axes[number], axis=dim, tiled=True)
    return filled


def joined_along(parts, dim):
    parts = jnp.moveaxis(parts, 0, dim)
    shape = parts.shape
    return parts.reshape(*shape[:dim], shape[dim] * shape[dim + 1], *shape[dim + 2 :])


def from_everyone(x, axis):
    peers = lax.axis_size(axis)
    return lax.all_to_all(jnp.broadcast_to(x[None], (peers, *x.shape)), axis, 0, 0, tiled=True)


def collect(x, axis, dim):
    return joined_along(from_everyone(x, axis), dim)


def silu_slope(pre):
    sig = jax.nn.sigmoid(pre)
    return sig * (1.0 + pre * (1.0 - sig))


def finish_forward(tokens, targets, pre, down_whole, inv_hidden):
    hidden_act = jax.nn.silu(pre).astype(jnp.bfloat16)
    mixed = (
        lax.dot_general(
            hidden_act, down_whole, (((1,), (1,)), ((), ())), preferred_element_type=jnp.float32
        )
        * inv_hidden
    )
    slope_out = (tokens.astype(jnp.float32) + mixed - targets.astype(jnp.float32)).astype(
        jnp.bfloat16
    )
    return (hidden_act, slope_out)


def packed(grad, rate):
    spread = jnp.sqrt(jnp.mean(grad * grad, axis=-1, keepdims=True) + 1e-05)
    unit = grad / (jnp.abs(grad) + spread)
    largest = jnp.max(jnp.abs(unit), axis=-1, keepdims=True) + 1e-06
    return ((unit / largest).astype(jnp.bfloat16), rate * largest[..., 0])


def owner_sum(weights, pieces):
    quant, scales = pieces
    factor = weights[:, None] * scales
    return jnp.sum(factor[:, :, None] * quant.astype(jnp.float32), axis=0)


def per_device(
    tokens, targets, w_up, w_down, up_momentum, down_momentum, member_up, member_down, path_rate
):
    width = tokens.shape[1]
    hidden = w_up.shape[2]
    rows = tokens.shape[0]
    inv_width = width ** (-0.5)
    inv_hidden = hidden ** (-0.5)
    row_index = lax.axis_index(ROW)
    col_index = lax.axis_index("col")
    row_count = lax.axis_size(ROW)
    col_count = lax.axis_size("col")
    rates_up = lax.dynamic_index_in_dim(path_rate, col_index, 1, False)
    rates_down = lax.dynamic_index_in_dim(path_rate, row_index, 0, False)
    down_whole = lax.all_gather(w_down[0], "col", axis=0, tiled=True)
    up_whole = gathered_by_axis(w_up[0], ROW, 0)
    pre = jnp.dot(tokens, up_whole, preferred_element_type=jnp.float32) * inv_width
    hidden_act, slope_out = finish_forward(tokens, targets, pre, down_whole, inv_hidden)
    slope_hidden = jnp.dot(slope_out, down_whole, preferred_element_type=jnp.float32) * inv_hidden
    slope_pre = (slope_hidden * silu_slope(pre)).astype(jnp.bfloat16)
    flags_up = lax.dynamic_index_in_dim(member_up, col_index, 1, False).astype(jnp.float32)
    weights_up = flags_up / jnp.sum(flags_up)
    input_parts = lax.all_to_all(
        tokens.reshape(rows, row_count, width // row_count),
        ROW,
        split_axis=1,
        concat_axis=1,
        tiled=True,
    )
    slope_parts = collect(slope_pre[None], ROW, 0)
    grads_owned = (
        jnp.einsum("rsk,srh->skh", input_parts, slope_parts, preferred_element_type=jnp.float32)
        * inv_width
    )
    quant_owned, scales_owned = packed(grads_owned, rates_up[:, None])
    average_up = owner_sum(weights_up, (quant_owned, scales_owned))
    momentum_first = 0.9 * up_momentum[0] + average_up
    fresh_up = (w_up[0].astype(jnp.float32) - 0.7 * (average_up + 0.9 * momentum_first)).astype(
        jnp.bfloat16
    )
    fresh_whole = gathered_by_axis(fresh_up, ROW, 0)
    pre_again = jnp.dot(tokens, fresh_whole, preferred_element_type=jnp.float32) * inv_width
    hidden_again, slope_again = finish_forward(tokens, targets, pre_again, down_whole, inv_hidden)
    flags_down = lax.dynamic_index_in_dim(member_down, row_index, 0, False).astype(jnp.float32)
    weights_down = flags_down / jnp.sum(flags_down)
    output_parts = lax.all_to_all(
        slope_again.reshape(rows, col_count, width // col_count),
        "col",
        split_axis=1,
        concat_axis=1,
        tiled=True,
    )
    hidden_parts = lax.all_gather(hidden_again[None], "col", axis=0, tiled=True)
    grads_down = (
        jnp.einsum("rsk,srh->skh", output_parts, hidden_parts, preferred_element_type=jnp.float32)
        * inv_hidden
    )
    quant_down, scales_down = packed(grads_down, rates_down[:, None])
    average_down = owner_sum(weights_down, (quant_down, scales_down))
    momentum_second = 0.9 * down_momentum[0] + average_down
    fresh_down = (
        w_down[0].astype(jnp.float32) - 0.7 * (average_down + 0.9 * momentum_second)
    ).astype(jnp.bfloat16)
    return (fresh_up[None], momentum_first[None], fresh_down[None], momentum_second[None])


def solution(mesh):
    torus = Mesh(mesh.devices.reshape(8, 2, mesh.shape["col"]), ("row_0", "row_1", "col"))
    placed = (
        P(ROW_COL, None),
        P(ROW_COL, None),
        P("col", ROW, None),
        P(ROW, "col", None),
        P("col", ROW, None),
        P(ROW, "col", None),
        P(),
        P(),
        P(),
    )
    return jax.shard_map(
        per_device,
        mesh=torus,
        in_specs=placed,
        out_specs=(
            P("col", ROW, None),
            P("col", ROW, None),
            P(ROW, "col", None),
            P(ROW, "col", None),
        ),
        check_vma=False,
    )
```

profile of v0, /device:TPU:1, one launch (start us, length us, event | category | flops | bytes accessed | tf_op | source)
XLA Modules:
  0.0 421.4 jit_solution(14377181742692491667)
XLA Ops:
  7.2 8.2 %all-gather = bf16[1,448,448]{2,1,0:T(8,128)(2,1)} all-gather(bf16[1,224,448]{2,1,0:T(8,128)(2,1)} %param.11), channel_id=2, replica_groups=mesh['row_0'=8,'row_1'=2,'col'=32] {'row_1'}, dimensions={1}, use_global_device_ids=true | all-gather | bytes 602112 | tf_op jit(solution)/shard_map/all_gather | solution.py:14
  16.2 2.2 copy.27
  18.4 8.8 %all-to-all-start.1 = ((bf16[128,16,224]{0,2,1:T(8,128)(2,1)}), bf16[128,16,224]{0,2,1:T(8,128)(2,1)S(1)}, u32[]{:S(2)}, u32[]{:S(2)}) async-start(bf16[128,16,224]{0,2,1:T(8,128)(2,1)} %bitcast.3), calls=%async_computation.1 | async-start | bytes 1835008 | tf_op jit(solution)/shard_map/all_to_all | solution.py:87
  27.3 58.7 %all-gather.11.cloned.1.call-done = bf16[1,3584,448]{2,1,0:T(8,128)(2,1)} async-done(((bf16[1,448,448]{2,1,0:T(8,128)(2,1)}), bf16[1,3584,448]{2,1,0:T(8,128)(2,1)}) %all-gather.11.cloned.1.call-update) | async-done | bytes 3211280 | tf_op jit(solution)/shard_map/all_gather | solution.py:14
  86.0 3.8 fusion.25
  89.8 93.1 %all-gather.13.cloned.1.call-done = bf16[1,3584,448]{2,1,0:T(8,128)(2,1)} async-done(((bf16[1,112,448]{2,1,0:T(8,128)(2,1)}), bf16[1,3584,448]{2,1,0:T(8,128)(2,1)}) %all-gather.13.cloned.1.call-update) | async-done | bytes 3211280 | tf_op jit(solution)/shard_map/all_gather | solution.py:79
  182.9 5.3 %fusion.39 = bf16[128,448]{0,1:T(8,128)(2,1)S(1)} fusion(bf16[1,3584,448]{2,1,0:T(8,128)(2,1)} %all-gather.13.cloned.1.call-done, bf16[128,3584]{1,0:T(8,128)(2,1)S(1)} %copy-done.2, bf16[128,3584]{1,0:T(8,128)(2,1)S(1)} %copy-done, f32[128,448]{0,1:T(8,128)S(1)} %fusion.25), kind=kOutput, calls=%fused_computation.40 | convolution fusion | flops 825696256 | bytes 5390336 | tf_op jit(solution)/shard_map/dot_general | solution.py:83
  188.3 1.6 broadcast_in_dim.4
  189.9 6.6 %all-to-all-start = ((bf16[16,1,128,448]{2,3,1,0:T(8,128)(2,1)}), bf16[16,1,128,448]{2,3,1,0:T(8,128)(2,1)S(1)}, u32[]{:S(2)}, u32[]{:S(2)}) async-start(bf16[16,1,128,448]{2,3,1,0:T(8,128)(2,1)} %broadcast_in_dim.4), calls=%async_computation | async-start | bytes 3670016 | tf_op jit(solution)/shard_map/all_to_all | solution.py:26
  200.3 39.1 %all-to-all-done = bf16[16,1,128,448]{2,3,1,0:T(8,128)(2,1)S(1)} async-done(((bf16[16,1,128,448]{2,3,1,0:T(8,128)(2,1)}), bf16[16,1,128,448]{2,3,1,0:T(8,128)(2,1)S(1)}, u32[]{:S(2)}, u32[]{:S(2)}) %all-to-all-start) | async-done | bytes 1835040 | tf_op jit(solution)/shard_map/all_to_all | solution.py:26
  239.4 2.3 fusion.2
  241.7 2.0 fusion.5
  243.8 2.4 multiply_reduce_fusion.2
  246.5 5.7 %all_gather.21 = bf16[448,448]{1,0:T(8,128)(2,1)} all-gather(bf16[224,448]{1,0:T(8,128)(2,1)S(1)} %copy.29), channel_id=1, replica_groups=mesh['row_0'=8,'row_1'=2,'col'=32] {'row_1'}, dimensions={0}, use_global_device_ids=true | all-gather | bytes 602112 | tf_op jit(solution)/shard_map/all_gather | solution.py:14
  252.4 50.7 %all-gather.9.cloned.1.call-done = bf16[3584,448]{1,0:T(8,128)(2,1)} async-done(((bf16[448,448]{1,0:T(8,128)(2,1)}), bf16[3584,448]{1,0:T(8,128)(2,1)}) %all-gather.9.cloned.1.call-update) | async-done | bytes 3211280 | tf_op jit(solution)/shard_map/all_gather | solution.py:14
  303.1 4.0 multiply_convert_fusion
  307.1 3.7 fusion.11
  312.2 10.6 %all-to-all-start.2 = ((bf16[128,32,112]{0,2,1:T(8,128)(2,1)}), bf16[128,32,112]{0,2,1:T(8,128)(2,1)S(1)}, u32[]{:S(2)}, u32[]{:S(2)}) async-start(bf16[128,32,112]{0,2,1:T(8,128)(2,1)} %bitcast.114), calls=%async_computation.2 | async-start | bytes 1835008 | tf_op jit(solution)/shard_map/all_to_all | solution.py:110
  324.1 1.3 fusion.67
  327.3 25.0 %all-to-all-done.2 = bf16[128,32,112]{0,2,1:T(8,128)(2,1)S(1)} async-done(((bf16[128,32,112]{0,2,1:T(8,128)(2,1)}), bf16[128,32,112]{0,2,1:T(8,128)(2,1)S(1)}, u32[]{:S(2)}, u32[]{:S(2)}) %all-to-all-start.2) | async-done | bytes 917536 | tf_op jit(solution)/shard_map/all_to_all | solution.py:110
  352.4 51.8 %all-gather.15.cloned.1.call-done = bf16[4096,448]{0,1:T(8,128)(2,1)} async-done(((bf16[128,448]{0,1:T(8,128)(2,1)}), bf16[4096,448]{0,1:T(8,128)(2,1)}) %all-gather.15.cloned.1.call-update) | async-done | bytes 3670032 | tf_op jit(solution)/shard_map/all_gather | solution.py:117
  404.2 3.8 multiply_reduce_fusion.1
  408.0 3.1 abs_reduce_fusion
  411.2 2.8 multiply_reduce_fusion
  (39 shorter events, 10.6 us)
Async XLA Ops:
  7.2 175.8 %copy-start = (bf16[128,3584]{1,0:T(8,128)(2,1)S(1)}, bf16[128,3584]{1,0:T(8,128)(2,1)}, u32[]{:S(2)}) copy-start(bf16[128,3584]{1,0:T(8,128)(2,1)} %param.9) | copy-start | bytes 2752516
  7.2 175.8 %copy-start.2 = (bf16[128,3584]{1,0:T(8,128)(2,1)S(1)}, bf16[128,3584]{1,0:T(8,128)(2,1)}, u32[]{:S(2)}) copy-start(bf16[128,3584]{1,0:T(8,128)(2,1)} %param.10) | copy-start | bytes 2752516
  7.2 78.8 %all-gather.11.cloned.1.call-start = ((), (), s32[]{:S(2)}) async-start(), calls=%async_computation.4 | async-start | bytes 4128768 | tf_op jit(solution)/shard_map/all_gather | solution.py:14
  15.5 167.5 %all-gather.13.cloned.1.call-start = ((), (), s32[]{:S(2)}) async-start(), calls=%async_computation.5 | async-start | bytes 3784704 | tf_op jit(solution)/shard_map/all_gather | solution.py:79
  18.4 169.8 %all-to-all-start.1 = ((bf16[128,16,224]{0,2,1:T(8,128)(2,1)}), bf16[128,16,224]{0,2,1:T(8,128)(2,1)S(1)}, u32[]{:S(2)}, u32[]{:S(2)}) async-start(bf16[128,16,224]{0,2,1:T(8,128)(2,1)} %bitcast.3), calls=%async_computation.1 | async-start | bytes 1835008 | tf_op jit(solution)/shard_map/all_to_all | solution.py:87
  89.8 109.0 %copy-start.5 = (s32[16,32]{1,0:T(8,128)S(1)}, s32[16,32]{1,0:T(8,128)}, u32[]{:S(2)}) copy-start(s32[16,32]{1,0:T(8,128)} %param.15) | copy-start | bytes 6148
  89.8 109.7 %copy-start.6 = (f32[16,32]{1,0:T(8,128)S(1)}, f32[16,32]{1,0:T(8,128)}, u32[]{:S(2)}) copy-start(f32[16,32]{1,0:T(8,128)} %param.17) | copy-start | bytes 6148
  188.3 1.6 copy-start.1
  189.9 49.5 %all-to-all-start = ((bf16[16,1,128,448]{2,3,1,0:T(8,128)(2,1)}), bf16[16,1,128,448]{2,3,1,0:T(8,128)(2,1)S(1)}, u32[]{:S(2)}, u32[]{:S(2)}) async-start(bf16[16,1,128,448]{2,3,1,0:T(8,128)(2,1)} %broadcast_in_dim.4), calls=%async_computation | async-start | bytes 3670016 | tf_op jit(solution)/shard_map/all_to_all | solution.py:26
  196.4 106.7 %all-gather.9.cloned.1.call-start = ((), (), s32[]{:S(2)}) async-start(), calls=%async_computation.3 | async-start | bytes 4128768 | tf_op jit(solution)/shard_map/all_gather | solution.py:14
  252.2 152.0 %all-gather.15.cloned.1.call-start = ((), (), s32[]{:S(2)}) async-start(), calls=%async_computation.6 | async-start | bytes 3784704 | tf_op jit(solution)/shard_map/all_gather | solution.py:117
  312.2 40.2 %all-to-all-start.2 = ((bf16[128,32,112]{0,2,1:T(8,128)(2,1)}), bf16[128,32,112]{0,2,1:T(8,128)(2,1)S(1)}, u32[]{:S(2)}, u32[]{:S(2)}) async-start(bf16[128,32,112]{0,2,1:T(8,128)(2,1)} %bitcast.114), calls=%async_computation.2 | async-start | bytes 1835008 | tf_op jit(solution)/shard_map/all_to_all | solution.py:110
  408.0 6.1 %copy-start.3 = (bf16[1,112,448]{2,1,0:T(8,128)(2,1)S(1)}, bf16[1,112,448]{2,1,0:T(8,128)(2,1)}, u32[]{:S(2)}) copy-start(bf16[1,112,448]{2,1,0:T(8,128)(2,1)} %param.12) | copy-start | bytes 301060
  408.0 6.1 %copy-start.4 = (f32[1,112,448]{2,1,0:T(8,128)S(1)}, f32[1,112,448]{2,1,0:T(8,128)}, u32[]{:S(2)}) copy-start(f32[1,112,448]{2,1,0:T(8,128)} %param.14) | copy-start | bytes 602116
Sparse Core Ops, SparseCore 0:
  15.6 70.3 all-gather.10
  89.3 93.5 all-gather.12
  252.3 50.7 all-gather.8
  307.3 96.8 all-gather.14
where the time goes:
time: 422 us; the launch traced here: 421 us
  waiting for transfers between devices  319 us (76%)
  starting transfers between devices  26.4 us (6%)
  matrix products  23 us (5%)
  other arithmetic  15.7 us (4%)
  between operations  14 us (3%)
  blocking collectives  13.9 us (3%)
  local copies, waits for them, and re-layouts  9.32 us (2%)
    all_gather x2, waiting for transfers between devices, gathered_by_axis(): filled = lax.all_gather(filled, axes[number], axis=dim, tiled=True)  109 us
    all_gather x1, waiting for transfers between devices, per_device(): down_whole = lax.all_gather(w_down[0], 'col', axis=0, tiled=True)  93.1 us
    all_gather x1, waiting for transfers between devices, per_device(): hidden_parts = lax.all_gather(hidden_again[None], 'col', axis=0, tiled=True)  51.8 us
    all_to_all x1, waiting for transfers between devices, from_everyone(): lax.all_to_all(jnp.broadcast_to(x[None], (peers, *x.shape)), axis, 0, 0,...  39.1 us
    all_to_all x1, waiting for transfers between devices, per_device(): lax.all_to_all(slope_again.reshape(rows, col_count, width // col_count),...  25 us
    all_gather x2, blocking collectives, gathered_by_axis(): filled = lax.all_gather(filled, axes[number], axis=dim, tiled=True)  13.9 us
    all_to_all x1, starting transfers between devices, per_device(): lax.all_to_all(slope_again.reshape(rows, col_count, width // col_count),...  10.6 us
    all_to_all x1, starting transfers between devices, per_device(): lax.all_to_all(tokens.reshape(rows, row_count, width // row_count), ROW,...  8.84 us
  transfers between devices with their start and end apart: 7, of which 6 were waited for; matrix products, arithmetic and copies ran while one was open for 6% of the time, Pallas kernels for 0%

commit v1 on v0

v1 whole, which is shorter than its diff:
```python
import jax
import jax.numpy as jnp
from jax import lax
from jax.experimental import pallas as pl
from jax.experimental.pallas import tpu as pltpu
from jax.sharding import Mesh
from jax.sharding import PartitionSpec as P

MESH = pl.DeviceIdType.MESH
F32 = jnp.float32
BF16 = jnp.bfloat16
AXES = {"y": 8, "xl": 2, "xh": 2, "z": 8, "core": 2}
ROW = ("y", "xl")
COL = ("xh", "z", "core")
N_ROW, N_COL = 16, 32
NT = (((1,), (1,)), ((), ()))


def shifted(axis, step):
    size = AXES[axis]
    return lax.rem(lax.axis_index(axis) + (step % size), size)


class Mail:
    def __init__(self, send_sems, recv_sems):
        self.send_sems, self.recv_sems = send_sems, recv_sems
        self.number = {}
        self.sent = []

    def copy(self, key, ref, device):
        number = self.number.setdefault(key, len(self.number))
        return pltpu.make_async_remote_copy(
            src_ref=ref[0],
            dst_ref=ref[1],
            send_sem=self.send_sems.at[number],
            recv_sem=self.recv_sems.at[number],
            device_id=device,
            device_id_type=MESH,
        )

    def send(self, key, src, dst, **steps):
        device = {axis: shifted(axis, step) for axis, step in steps.items()}
        copy = self.copy(key, (src, dst), device)
        copy.start()
        self.sent.append(copy)

    def wait(self, key, slot, axis):
        self.copy(key, (slot, slot), {axis: shifted(axis, 1)}).wait_recv()

    def finish(self):
        for copy in self.sent:
            copy.wait_send()


def gather_balanced(mail, name, slot, line, pair, arrived):
    def send(key, dl, dp, h, **steps):
        ref = slot(dl, dp, h)
        mail.send((name, *key, h), ref, ref, **steps)

    def wait(key, dl, dp, h, axis):
        mail.wait((name, *key, h), slot(dl, dp, h), axis)

    ways = (1, -1)
    for h in (0, 1):
        for way in ways:
            send(("l", way, 1, 0), 0, 0, h, **{line: way})
        send(("p", 0, 0), 0, 0, h, **{pair: 1})
    arrived(0, 0)
    yield
    for h in (0, 1):
        for way in ways:
            wait(("l", way, 1, 0), -way, 0, h, line)
            send(("l", way, 2, 0), -way, 0, h, **{line: way})
            send(("p", way, 1), -way, 0, h, **{pair: 1})
    for way in ways:
        arrived(-way, 0)
    yield
    for h in (0, 1):
        for way in ways:
            wait(("l", way, 2, 0), -2 * way, 0, h, line)
            send(("l", way, 3, 0), -2 * way, 0, h, **{line: way})
            send(("p", way, 2), -2 * way, 0, h, **{pair: 1})
    for h in (0, 1):
        wait(("p", 0, 0), 0, 1, h, pair)
    for way in ways:
        arrived(-2 * way, 0)
    arrived(0, 1)
    yield
    for h in (0, 1):
        for way in ways:
            wait(("l", way, 3, 0), -3 * way, 0, h, line)
            if way == 1 - 2 * h:
                send(("l", way, 4, 0), -3 * way, 0, h, **{line: way})
        for way in ways:
            wait(("p", way, 2), -2 * way, 1, h, pair)
            send(("l", way, 3, 1), -2 * way, 1, h, **{line: way})
    for h in (0, 1):
        for way in ways:
            wait(("p", way, 1), -way, 1, h, pair)
    for way in ways:
        arrived(-3 * way, 0)
        arrived(-2 * way, 1)
        arrived(-way, 1)
    yield
    for h in (0, 1):
        way = 1 - 2 * h
        wait(("l", way, 3, 1), -3 * way, 1, h, line)
        send(("l", way, 4, 1), -3 * way, 1, h, **{line: way})
    for h in (0, 1):
        way = 2 * h - 1
        wait(("l", way, 3, 1), -3 * way, 1, h, line)
    for way in ways:
        arrived(-3 * way, 1)
    for h in (0, 1):
        way = 1 - 2 * h
        wait(("l", way, 4, 0), -4 * way, 0, h, line)
    arrived(4, 0)
    for h in (0, 1):
        way = 1 - 2 * h
        wait(("l", way, 4, 1), -4 * way, 1, h, line)
    arrived(4, 1)
    yield


def gather_line(mail, name, slot, line, pair, arrived):
    def send(key, dl, dp, **steps):
        ref = slot(dl, dp)
        mail.send((name, *key), ref, ref, **steps)

    def wait(key, dl, dp, axis):
        mail.wait((name, *key), slot(dl, dp), axis)

    ways = (1, -1)
    send(("p",), 0, 0, **{pair: 1})
    for way in ways:
        send(("l", way, 1, 0), 0, 0, **{line: way})
    arrived(0, 0)
    yield
    wait(("p",), 0, 1, pair)
    for way in ways:
        send(("l", way, 1, 1), 0, 1, **{line: way})
    arrived(0, 1)
    for d in (1, 2, 3):
        yield
        for dp in (0, 1):
            for way in ways:
                wait(("l", way, d, dp), -d * way, dp, line)
                if d < 3 or way == 1 - 2 * dp:
                    send(("l", way, d + 1, dp), -d * way, dp, **{line: way})
                arrived(-d * way, dp)
    yield
    for dp in (0, 1):
        wait(("l", 1 - 2 * dp, 4, dp), 4, dp, line)
        arrived(4, dp)
    yield


def packed_sum(grad, weight):
    size = jnp.abs(grad)
    spread = jnp.sqrt(jnp.mean(grad * grad, axis=-1, keepdims=True) + 1e-05)
    top = jnp.max(size, axis=-1, keepdims=True)
    largest = top / (top + spread) + 1e-06
    quant = (grad / ((size + spread) * largest)).astype(BF16)
    return quant.astype(F32) * (weight * largest)


def kernel(
    x_ref,
    t_ref,
    wu_ref,
    wd_ref,
    mu_ref,
    md_ref,
    member_up,
    member_down,
    path_rate,
    new_up,
    new_mu,
    new_down,
    new_md,
    up_all,
    down_all,
    fresh_all,
    x_out,
    x_in,
    d_out,
    d_in,
    dpre_all,
    hid_all,
    dh_ref,
    acc_up,
    acc_down,
    send_sems,
    recv_sems,
    local_sems,
):
    rows, width = x_ref.shape
    hidden = wu_ref.shape[1]
    inv_width = width ** (-0.5)
    inv_hidden = hidden ** (-0.5)
    own_up, own_down = wu_ref.shape[0], wd_ref.shape[0]
    step = 512
    steps = width // step
    y, xl = lax.axis_index("y"), lax.axis_index("xl")
    xh, z, core = lax.axis_index("xh"), lax.axis_index("z"), lax.axis_index("core")
    row = y * 2 + xl
    col = xh * 16 + z * 2 + core

    row_peers = [
        (dl, dp) for dl in (4, 3, -3, 2, -2, 1, -1, 0) for dp in (1, 0) if (dl, dp) != (0, 0)
    ]
    col_peers = [
        (dl, dp, dc)
        for dl in (4, 3, -3, 2, -2, 1, -1, 0)
        for dp in (1, 0)
        for dc in (1, 0)
        if (dl, dp, dc) != (0, 0, 0)
    ]

    barrier = pltpu.get_barrier_semaphore()
    for dl, dp in row_peers:
        pl.semaphore_signal(
            barrier,
            inc=1,
            device_id={"y": shifted("y", dl), "xl": shifted("xl", dp)},
            device_id_type=MESH,
        )
    for dl, dp, dc in col_peers:
        pl.semaphore_signal(
            barrier,
            inc=1,
            device_id={
                "z": shifted("z", dl),
                "xh": shifted("xh", dp),
                "core": shifted("core", dc),
            },
            device_id_type=MESH,
        )

    def row_of(dl, dp):
        return shifted("y", dl) * 2 + shifted("xl", dp)

    def col_of(dl, dp, dc):
        return shifted("xh", dp) * 16 + shifted("z", dl) * 2 + shifted("core", dc)

    def cut(ref, number, size, start=0, length=None):
        length = size if length is None else length
        return ref.at[pl.ds(pl.multiple_of(number * size + start, 16), length)]

    def nothing(dl, dp):
        pass

    mail = Mail(send_sems, recv_sems)
    half_up, half_hid = own_up // 2, hidden // 2

    own_copies = [
        pltpu.make_async_copy(wu_ref, cut(up_all, row, own_up), local_sems.at[0]),
        pltpu.make_async_copy(wd_ref, cut(down_all, col, own_down), local_sems.at[1]),
    ]
    for copy in own_copies:
        copy.start()
    for copy in own_copies:
        copy.wait()

    pl.semaphore_wait(barrier, len(row_peers) + len(col_peers))

    def up_slot(dl, dp, h):
        return cut(up_all, row_of(dl, dp), own_up, h * half_up, half_up)

    def fresh_slot(dl, dp, h):
        return cut(fresh_all, row_of(dl, dp), own_up, h * half_up, half_up)

    def down_slot(dl, dp, dc=0):
        return cut(down_all, col_of(dl, dp, dc), own_down)

    def dpre_slot(dl, dp, h):
        return dpre_all.at[row_of(dl, dp), pl.ds(h * half_hid, half_hid)]

    def hid_slot(dl, dp, h):
        return hid_all.at[col_of(dl, dp, 0), pl.ds(h * half_hid, half_hid)]

    def hid_whole(dl, dp, dc):
        return hid_all.at[col_of(dl, dp, dc)]

    def down_arrived(dl, dp):
        ref = down_slot(dl, dp)
        mail.send(("down sibling", dl % 8, dp), ref, ref, core=1)

    def hid_arrived(dl, dp):
        ref = hid_whole(dl, dp, 0)
        mail.send(("hid sibling", dl % 8, dp), ref, ref, core=1)

    pairs = [(dl, dp) for dl in range(8) for dp in range(2)]

    up_steps = gather_balanced(mail, "up", up_slot, "y", "xl", nothing)
    down_steps = gather_line(mail, "down", down_slot, "z", "xh", down_arrived)
    next(up_steps)
    next(down_steps)

    def turn(j, carry):
        at = pl.multiple_of(j * 128, 128)
        tile = x_ref[:, pl.ds(at, 128)].astype(F32)
        x_out[pl.ds(at, 128), :] = tile.T.astype(BF16)
        other = t_ref[:, pl.ds(at, 128)].astype(F32)
        d_out[pl.ds(at, 128), :] = (tile - other).T.astype(BF16)
        return carry

    lax.fori_loop(0, width // 128, turn, 0)
    next(up_steps)
    next(down_steps)
    next(up_steps)
    next(down_steps)
    next(up_steps)
    for dl, dp in row_peers:
        mail.send(
            ("tokens", dl % 8, dp),
            cut(x_out, row_of(dl, dp), own_up),
            cut(x_in, row, own_up),
            y=dl,
            xl=dp,
        )
    next(down_steps)
    next(up_steps)
    next(down_steps)
    for dl, dp, dc in col_peers:
        mail.send(
            ("delta", dl % 8, dp, dc),
            cut(d_out, col_of(dl, dp, dc), own_down),
            cut(d_in, col, own_down),
            z=dl,
            xh=dp,
            core=dc,
        )
    next(down_steps)
    x_in[pl.ds(pl.multiple_of(row * own_up, 16), own_up), :] = x_out[
        pl.ds(pl.multiple_of(row * own_up, 16), own_up), :
    ]
    d_in[pl.ds(pl.multiple_of(col * own_down, 16), own_down), :] = d_out[
        pl.ds(pl.multiple_of(col * own_down, 16), own_down), :
    ]

    def project(weights):
        def body(k, total):
            at = pl.multiple_of(k * step, step)
            return total + jnp.dot(
                x_ref[:, pl.ds(at, step)],
                weights[pl.ds(at, step), :],
                preferred_element_type=F32,
            )

        return lax.fori_loop(0, steps, body, jnp.zeros((rows, hidden), F32)) * inv_width

    pre = project(up_all)
    sig = jax.nn.sigmoid(pre)
    hid = (pre * sig).astype(BF16)
    slope = sig * (1.0 + pre * (1.0 - sig))
    for dl, dp in pairs:
        mail.wait(("down sibling", dl, dp), down_slot(dl, dp, 1), "core")

    dh_ref[...] = jnp.zeros_like(dh_ref)

    def back(k, carry):
        at = pl.multiple_of(k * step, step)
        part = down_all[pl.ds(at, step), :]
        mixed = lax.dot_general(hid, part, NT, preferred_element_type=F32) * inv_hidden
        dy = (
            x_ref[:, pl.ds(at, step)].astype(F32) + mixed - t_ref[:, pl.ds(at, step)].astype(F32)
        ).astype(BF16)
        dh_ref[...] += jnp.dot(dy, part, preferred_element_type=F32)
        return carry

    lax.fori_loop(0, steps, back, 0)
    dpre = dh_ref[...] * inv_hidden * slope
    dpre_all[row] = dpre.T.astype(BF16)

    for _ in gather_balanced(mail, "dpre", dpre_slot, "y", "xl", nothing):
        pass
    for dl, dp in row_peers:
        mail.wait(("tokens", dl % 8, dp), cut(x_in, row_of(-dl, dp), own_up), "y")

    acc_up[...] = jnp.zeros_like(acc_up)

    def up_path(p, count):
        at = pl.multiple_of(p * own_up, 16)
        grad = (
            lax.dot_general(
                x_in[pl.ds(at, own_up), :], dpre_all[p], NT, preferred_element_type=F32
            )
            * inv_width
        )
        flag = member_up[p, col].astype(F32)
        acc_up[...] += packed_sum(grad, flag * path_rate[p, col])
        return count + flag

    count_up = lax.fori_loop(0, N_ROW, up_path, jnp.float32(0.0))
    average = acc_up[...] / count_up
    momentum = 0.9 * mu_ref[...] + average
    new_mu[...] = momentum
    fresh = (wu_ref[...].astype(F32) - 0.7 * (average + 0.9 * momentum)).astype(BF16)
    new_up[...] = fresh
    fresh_all[pl.ds(pl.multiple_of(row * own_up, 16), own_up), :] = fresh

    for _ in gather_balanced(mail, "fresh", fresh_slot, "y", "xl", nothing):
        pass
    pre_again = project(fresh_all)
    hid_again = pre_again * jax.nn.sigmoid(pre_again)
    hid_all[col] = hid_again.T.astype(BF16)

    for _ in gather_balanced(mail, "hid", hid_slot, "z", "xh", hid_arrived):
        pass
    for dl, dp, dc in col_peers:
        mail.wait(("delta", dl % 8, dp, dc), cut(d_in, col_of(-dl, dp, dc), own_down), "z")
    for dl, dp in pairs:
        mail.wait(("hid sibling", dl, dp), hid_whole(dl, dp, 1), "core")

    acc_down[...] = jnp.zeros_like(acc_down)

    def down_path(q, count):
        at = pl.multiple_of(q * own_down, 16)
        acts = hid_all[q]
        mixed = jnp.dot(wd_ref[...], acts, preferred_element_type=F32) * inv_hidden
        dy = (d_in[pl.ds(at, own_down), :].astype(F32) + mixed).astype(BF16)
        grad = lax.dot_general(dy, acts, NT, preferred_element_type=F32) * inv_hidden
        flag = member_down[row, q].astype(F32)
        acc_down[...] += packed_sum(grad, flag * path_rate[row, q])
        return count + flag

    count_down = lax.fori_loop(0, N_COL, down_path, jnp.float32(0.0))
    average_down = acc_down[...] / count_down
    momentum_down = 0.9 * md_ref[...] + average_down
    new_md[...] = momentum_down
    new_down[...] = (
        wd_ref[...].astype(F32) - 0.7 * (average_down + 0.9 * momentum_down)
    ).astype(BF16)
    mail.finish()


def per_device(
    tokens, targets, w_up, w_down, up_momentum, down_momentum, member_up, member_down, path_rate
):
    rows, width = tokens.shape
    own_up, hidden = w_up.shape[1:]
    own_down = w_down.shape[1]
    vmem = pl.BlockSpec(memory_space=pltpu.VMEM)
    smem = pl.BlockSpec(memory_space=pltpu.SMEM)
    messages = 256
    outs = pl.pallas_call(
        kernel,
        out_shape=(
            jax.ShapeDtypeStruct((own_up, hidden), BF16),
            jax.ShapeDtypeStruct((own_up, hidden), F32),
            jax.ShapeDtypeStruct((own_down, hidden), BF16),
            jax.ShapeDtypeStruct((own_down, hidden), F32),
        ),
        in_specs=[vmem] * 6 + [smem] * 3,
        out_specs=(vmem,) * 4,
        scratch_shapes=[
            pltpu.VMEM((width, hidden), BF16),
            pltpu.VMEM((width, hidden), BF16),
            pltpu.VMEM((width, hidden), BF16),
            pltpu.VMEM((width, rows), BF16),
            pltpu.VMEM((width, rows), BF16),
            pltpu.VMEM((width, rows), BF16),
            pltpu.VMEM((width, rows), BF16),
            pltpu.VMEM((N_ROW, hidden, rows), BF16),
            pltpu.VMEM((N_COL, hidden, rows), BF16),
            pltpu.VMEM((rows, hidden), F32),
            pltpu.VMEM((own_up, hidden), F32),
            pltpu.VMEM((own_down, hidden), F32),
            pltpu.SemaphoreType.DMA((messages,)),
            pltpu.SemaphoreType.DMA((messages,)),
            pltpu.SemaphoreType.DMA((2,)),
        ],
        compiler_params=pltpu.CompilerParams(
            collective_id=0, has_side_effects=True, vmem_limit_bytes=56 * 1024 * 1024
        ),
        name="path_mixture",
    )(
        tokens,
        targets,
        w_up[0],
        w_down[0],
        up_momentum[0],
        down_momentum[0],
        member_up,
        member_down,
        path_rate,
    )
    return tuple(out[None] for out in outs)


def solution(mesh):
    torus = Mesh(mesh.devices.reshape(tuple(AXES.values())), tuple(AXES))
    placed = (
        P(ROW + COL, None),
        P(ROW + COL, None),
        P(COL, ROW, None),
        P(ROW, COL, None),
        P(COL, ROW, None),
        P(ROW, COL, None),
        P(),
        P(),
        P(),
    )
    return jax.shard_map(
        per_device,
        mesh=torus,
        in_specs=placed,
        out_specs=(
            P(COL, ROW, None),
            P(COL, ROW, None),
            P(ROW, COL, None),
            P(ROW, COL, None),
        ),
        check_vma=False,
    )
```

time: 422 us -> 205 us (0.49)
  waiting for transfers between devices: 319 us -> 0 us
  Pallas kernels: 0 us -> 200 us
  starting transfers between devices: 26.4 us -> 0 us
  matrix products: 23 us -> 0 us
  other arithmetic: 15.7 us -> 0 us
  blocking collectives: 13.9 us -> 0 us
  between operations: 14 us -> 0.65 us
  local copies, waits for them, and re-layouts: 9.32 us -> 4.36 us
    all_gather x4 -> x0, waiting for transfers between devices: 254 us -> none  [the longest x2 109 us: gathered_by_axis(): filled = lax.all_gather(filled, axes[number], axis=dim, tiled=True)]
    pallas_call x0 -> x1, Pallas kernels: none -> 200 us  [per_device(): pl.pallas_call(kernel, out_shape=(jax.ShapeDtypeStruct((own_up, hidden),...]
    all_to_all x3 -> x0, waiting for transfers between devices: 64.1 us -> none  [the longest x1 39.1 us: from_everyone(): lax.all_to_all(jnp.broadcast_to(x[None], (peers, *x.shape)), axis, 0, 0,...]
    all_to_all x3 -> x0, starting transfers between devices: 26 us -> none  [the longest x1 10.6 us: per_device(): lax.all_to_all(slope_again.reshape(rows, col_count, width // col_count),...]
    dot_general x6 -> x0, matrix products: 23 us -> none  [the longest x1 5.31 us: per_device(): jnp.dot(slope_out, down_whole, preferred_element_type=jnp.float32)]
    all_gather x2 -> x0, blocking collectives: 13.9 us -> none  [gathered_by_axis(): filled = lax.all_gather(filled, axes[number], axis=dim, tiled=True)]
    reduce_sum x4 -> x0, other arithmetic: 7.18 us -> none  [the longest x2 5.2 us: owner_sum(): return jnp.sum(factor[:, :, None] * quant.astype(jnp.float32), axis=0)]
    reduce_max x2 -> x0, other arithmetic: 5.14 us -> none  [packed(): largest = jnp.max(jnp.abs(unit), axis=-1, keepdims=True) + 1e-06]
  transfers between devices with their start and end apart: 7 -> 0, of which waited for: 6 -> 0; matrix products, arithmetic and copies ran while one was open for 6% -> 0% of each run, Pallas kernels for 0% -> 0%
where the time goes in v1:
time: 205 us
  Pallas kernels  200 us (98%)
  local copies, waits for them, and re-layouts  4.36 us (2%)
    pallas_call x1, Pallas kernels, per_device(): pl.pallas_call(kernel, out_shape=(jax.ShapeDtypeStruct((own_up, hidden),...  200 us
    unnamed x10, local copies, waits for them, and re-layouts  4.36 us

profile of v1, /device:TPU:1, one launch (start us, length us, event | category | flops | bytes accessed | tf_op | source)
XLA Modules:
  0.0 205.1 jit_solution(18066247993152458266)
XLA Ops:
  0.6 200.1 %path_mixture.1 = (bf16[224,448]{1,0:T(8,128)(2,1)}, f32[224,448]{1,0:T(8,128)}, bf16[112,448]{1,0:T(8,128)(2,1)}, f32[112,448]{1,0:T(8,128)}) custom-call(bf16[128,3584]{1,0:T(8,128)(2,1)} %x_ref.1, bf16[128,3584]{1,0:T(8,128)(2,1)} %t_ref.1, bf16[224,448]{1,0:T(8,128)(2,1)} %bitcast.10, bf16[112,448]{1,0:T(8,128)(2,1)} %bitcast.15, f32[224,448]{1,0:T(8,128)} %bitcast.9, ...), custom_call_target="tpu_custom_call" | custom-call | tf_op jit(solution)/shard_map/path_mixture/pallas_call | solution.py:447
  200.7 0.0 copy-start
  200.7 1.7 copy.17
  202.4 0.0 copy-done
  202.4 0.0 copy-start.2
  202.4 0.8 copy.18
  203.2 0.2 copy-done.2
  203.4 0.0 copy-start.1
  203.4 0.6 copy.19
  204.1 0.3 copy-done.1
  204.4 0.7 copy.20
Async XLA Ops:
  200.7 1.7 copy-start
  202.4 1.0 copy-start.2
  203.4 1.0 copy-start.1

commit v2 on v1

v2 whole, which is shorter than its diff:
```python
import functools

import jax
import jax.numpy as jnp
from jax import lax
from jax.experimental import pallas as pl
from jax.experimental.pallas import tpu as pltpu
from jax.sharding import Mesh
from jax.sharding import PartitionSpec as P

MESH = pl.DeviceIdType.MESH
F32 = jnp.float32
BF16 = jnp.bfloat16
AXES = {"y": 8, "xl": 2, "xh": 2, "z": 8, "core": 2}
ROW = ("y", "xl")
COL = ("xh", "z", "core")
N_ROW, N_COL = 16, 32
NT = (((1,), (1,)), ((), ()))


def shifted(axis, step):
    size = AXES[axis]
    return lax.rem(lax.axis_index(axis) + (step % size), size)


class Mail:
    def __init__(self, send_sems, recv_sems):
        self.send_sems, self.recv_sems = send_sems, recv_sems
        self.number = {}
        self.sent = []

    def copy(self, key, ref, device):
        number = self.number.setdefault(key, len(self.number))
        return pltpu.make_async_remote_copy(
            src_ref=ref[0],
            dst_ref=ref[1],
            send_sem=self.send_sems.at[number],
            recv_sem=self.recv_sems.at[number],
            device_id=device,
            device_id_type=MESH,
        )

    def send(self, key, src, dst, **steps):
        device = {axis: shifted(axis, step) for axis, step in steps.items()}
        copy = self.copy(key, (src, dst), device)
        copy.start()
        self.sent.append(copy)

    def wait(self, key, slot, axis):
        self.copy(key, (slot, slot), {axis: shifted(axis, 1)}).wait_recv()

    def finish(self):
        for copy in self.sent:
            copy.wait_send()


def gather_balanced(mail, name, slot, line, pair):
    def send(key, dl, dp, h, **steps):
        ref = slot(dl, dp, h)
        mail.send((name, *key, h), ref, ref, **steps)

    def wait(key, dl, dp, h, axis):
        mail.wait((name, *key, h), slot(dl, dp, h), axis)

    ways = (1, -1)
    for h in (0, 1):
        for way in ways:
            send(("l", way, 1, 0), 0, 0, h, **{line: way})
        send(("p", 0, 0), 0, 0, h, **{pair: 1})
    yield
    for h in (0, 1):
        for way in ways:
            wait(("l", way, 1, 0), -way, 0, h, line)
            send(("l", way, 2, 0), -way, 0, h, **{line: way})
            send(("p", way, 1), -way, 0, h, **{pair: 1})
    yield
    for h in (0, 1):
        for way in ways:
            wait(("l", way, 2, 0), -2 * way, 0, h, line)
            send(("l", way, 3, 0), -2 * way, 0, h, **{line: way})
            send(("p", way, 2), -2 * way, 0, h, **{pair: 1})
    for h in (0, 1):
        wait(("p", 0, 0), 0, 1, h, pair)
    yield
    for h in (0, 1):
        for way in ways:
            wait(("l", way, 3, 0), -3 * way, 0, h, line)
            if way == 1 - 2 * h:
                send(("l", way, 4, 0), -3 * way, 0, h, **{line: way})
        for way in ways:
            wait(("p", way, 2), -2 * way, 1, h, pair)
            send(("l", way, 3, 1), -2 * way, 1, h, **{line: way})
    for h in (0, 1):
        for way in ways:
            wait(("p", way, 1), -way, 1, h, pair)
    yield
    for h in (0, 1):
        way = 1 - 2 * h
        wait(("l", way, 3, 1), -3 * way, 1, h, line)
        send(("l", way, 4, 1), -3 * way, 1, h, **{line: way})
    yield
    for h in (0, 1):
        way = 2 * h - 1
        wait(("l", way, 3, 1), -3 * way, 1, h, line)
    for dp in (0, 1):
        for h in (0, 1):
            way = 1 - 2 * h
            wait(("l", way, 4, dp), -4 * way, dp, h, line)
    yield


ORDER = (
    (0, 0),
    (-1, 0),
    (1, 0),
    (-2, 0),
    (2, 0),
    (0, 1),
    (-3, 0),
    (3, 0),
    (-2, 1),
    (2, 1),
    (-1, 1),
    (1, 1),
    (-3, 1),
    (3, 1),
    (4, 0),
    (4, 1),
)
READY = (None, (0, 3), (3, 6), (6, 9), (9, 12), (12, 16))


def picked(place, first, last, values):
    found = jnp.int32(values[first])
    for number in range(first + 1, last):
        found = jnp.where(place == number, jnp.int32(values[number]), found)
    return found


def scatter_balanced(mail, name, part, outgoing, incoming, kept, line, pair, result):
    places = {}

    def place(key):
        return places.setdefault(key, len(places))

    def send(key, value, **steps):
        at = place(key)
        outgoing[at] = value.astype(BF16)
        mail.send((name, *key), outgoing.at[at], incoming.at[at], **steps)

    def take(key, axis):
        at = place(key)
        mail.wait((name, *key), incoming.at[at], axis)
        return incoming[at].astype(F32)

    ways = (1, -1)
    for dp in (0, 1):
        for h in (0, 1):
            way = 1 - 2 * h
            send(("l", way, 4, dp, h), part(4, dp, h), **{line: way})
    yield
    for h in (0, 1):
        way = 2 * h - 1
        for dp in (0, 1):
            send(("l", way, 3, dp, h), part(3 * way, dp, h), **{line: way})
    for h in (0, 1):
        way = 1 - 2 * h
        for dp in (1, 0):
            total = part(3 * way, dp, h) + take(("l", way, 4, dp, h), line)
            send(("l", way, 3, dp, h), total, **{line: way})
    yield
    for h in (0, 1):
        for way in (2 * h - 1, 1 - 2 * h):
            total = part(2 * way, 1, h) + take(("l", way, 3, 1, h), line)
            send(("p", way, 2, h), total, **{pair: 1})
    for h in (0, 1):
        for way in (2 * h - 1, 1 - 2 * h):
            total = part(2 * way, 0, h) + take(("l", way, 3, 0, h), line)
            kept[2 * h + ways.index(way)] = total
    for h in (0, 1):
        for way in ways:
            send(("p", way, 1, h), part(way, 1, h), **{pair: 1})
    yield
    for h in (0, 1):
        for way in (2 * h - 1, 1 - 2 * h):
            total = kept[2 * h + ways.index(way)] + take(("p", way, 2, h), pair)
            send(("l", way, 2, h), total, **{line: way})
    for h in (0, 1):
        send(("p", 0, 0, h), part(0, 1, h), **{pair: 1})
    yield
    for h in (0, 1):
        for way in ways:
            total = part(way, 0, h) + take(("p", way, 1, h), pair)
            total = total + take(("l", way, 2, h), line)
            send(("l", way, 1, h), total, **{line: way})
    yield
    half = result.shape[0] // 2
    for h in (0, 1):
        total = part(0, 0, h) + take(("p", 0, 0, h), pair)
        for way in ways:
            total = total + take(("l", way, 1, h), line)
        result[pl.ds(h * half, half), :] = total
    yield


def gather_line(mail, name, slot, line, pair, arrived):
    def send(key, dl, dp, **steps):
        ref = slot(dl, dp)
        mail.send((name, *key), ref, ref, **steps)

    def wait(key, dl, dp, axis):
        mail.wait((name, *key), slot(dl, dp), axis)

    ways = (1, -1)
    send(("p",), 0, 0, **{pair: 1})
    for way in ways:
        send(("l", way, 1, 0), 0, 0, **{line: way})
    arrived(0, 0)
    yield
    wait(("p",), 0, 1, pair)
    for way in ways:
        send(("l", way, 1, 1), 0, 1, **{line: way})
    arrived(0, 1)
    for d in (1, 2, 3):
        yield
        for dp in (0, 1):
            for way in ways:
                wait(("l", way, d, dp), -d * way, dp, line)
                if d < 3 or way == 1 - 2 * dp:
                    send(("l", way, d + 1, dp), -d * way, dp, **{line: way})
                arrived(-d * way, dp)
    yield
    for dp in (0, 1):
        wait(("l", 1 - 2 * dp, 4, dp), 4, dp, line)
        arrived(4, dp)
    yield


def packed_sum(grad, weight):
    size = jnp.abs(grad)
    spread = jnp.sqrt(jnp.mean(grad * grad, axis=-1, keepdims=True) + 1e-05)
    top = jnp.max(size, axis=-1, keepdims=True)
    largest = top / (top + spread) + 1e-06
    quant = (grad / ((size + spread) * largest)).astype(BF16)
    return quant.astype(F32) * (weight * largest)


def kernel(
    x_hbm,
    t_hbm,
    wu_hbm,
    wd_hbm,
    mu_hbm,
    md_hbm,
    member_up,
    member_down,
    path_rate,
    new_up,
    new_mu,
    new_down,
    new_md,
    x_ref,
    t_ref,
    wu_ref,
    mu_ref,
    md_ref,
    turned,
    down_all,
    x_out,
    x_in,
    d_out,
    d_in,
    dpre_all,
    hid_all,
    dh_ref,
    pre_ref,
    kept,
    first_out,
    first_in,
    second_out,
    second_in,
    acc_up,
    acc_down,
    acc_sibling,
    send_sems,
    recv_sems,
    local_sems,
):
    rows, width = x_ref.shape
    own_up, hidden = wu_ref.shape
    own_down = md_ref.shape[0]
    inv_width = width ** (-0.5)
    inv_hidden = hidden ** (-0.5)
    step = 512
    steps = width // step
    y, xl = lax.axis_index("y"), lax.axis_index("xl")
    xh, z, core = lax.axis_index("xh"), lax.axis_index("z"), lax.axis_index("core")
    row = y * 2 + xl
    col = xh * 16 + z * 2 + core
    chip = xh * 8 + z

    peers = [(dl, dp) for dl in (4, 3, -3, 2, -2, 1, -1, 0) for dp in (1, 0) if dl or dp]
    barrier = pltpu.get_barrier_semaphore()
    for dl, dp in peers:
        for line, pair in (("y", "xl"), ("z", "xh")):
            pl.semaphore_signal(
                barrier,
                inc=1,
                device_id={line: shifted(line, dl), pair: shifted(pair, dp)},
                device_id_type=MESH,
            )
    pl.semaphore_signal(
        barrier, inc=1, device_id={"core": shifted("core", 1)}, device_id_type=MESH
    )

    def row_of(dl, dp):
        return lax.rem(y + (dl + 8), 8) * 2 + lax.rem(xl + dp, 2)

    def chip_of(dl, dp):
        return lax.rem(xh + dp, 2) * 8 + lax.rem(z + (dl + 8), 8)

    def col_of(dl, dp, dc):
        return chip_of(dl, dp) * 2 + lax.rem(core + dc, 2)

    def span(number, size):
        return pl.ds(pl.multiple_of(number * size, 16), size)

    def cut(ref, number, size):
        return ref.at[span(number, size)]

    mail = Mail(send_sems, recv_sems)
    half_hid = hidden // 2

    loads = [
        pltpu.make_async_copy(src, dst, local_sems.at[number])
        for number, (src, dst) in enumerate(
            (
                (x_hbm, x_ref),
                (wd_hbm, cut(down_all, col, own_down)),
                (wu_hbm, wu_ref),
                (t_hbm, t_ref),
                (mu_hbm, mu_ref),
                (md_hbm, md_ref),
            )
        )
    ]
    for load in loads:
        load.start()

    def down_slot(dl, dp, dc=0):
        return cut(down_all, col_of(dl, dp, dc), own_down)

    def dpre_slot(dl, dp, h):
        return dpre_all.at[row_of(dl, dp), pl.ds(h * half_hid, half_hid)]

    def hid_slot(dl, dp, h):
        return hid_all.at[chip_of(dl, dp), pl.ds(h * half_hid, half_hid)]

    def down_arrived(dl, dp):
        ref = down_slot(dl, dp)
        mail.send(("down sibling", dl % 8, dp), ref, ref, core=1)

    def send_delta(pairs):
        for dl, dp in peers:
            if dp in pairs:
                mail.send(
                    ("delta", dl % 8, dp),
                    cut(d_out, chip_of(dl, dp), 2 * own_down),
                    cut(d_in, chip, 2 * own_down),
                    z=dl,
                    xh=dp,
                )

    loads[0].wait()

    def turn(j, carry):
        at = pl.multiple_of(j * 128, 128)
        x_out[pl.ds(at, 128), :] = x_ref[:, pl.ds(at, 128)].astype(F32).T.astype(BF16)
        return carry

    lax.fori_loop(0, width // 128, turn, 0)
    loads[1].wait()
    pl.semaphore_wait(barrier, 2 * len(peers) + 1)
    for dl, dp in peers:
        mail.send(
            ("tokens", dl % 8, dp),
            cut(x_out, row_of(dl, dp), own_up),
            cut(x_in, row, own_up),
            y=dl,
            xl=dp,
        )
    down_steps = gather_line(mail, "down", down_slot, "z", "xh", down_arrived)
    next(down_steps)

    x_in[span(row, own_up), :] = x_out[span(row, own_up), :]
    loads[2].wait()
    turned[...] = wu_ref[...].astype(F32).T.astype(BF16)
    loads[3].wait()

    def turn_delta(j, carry):
        at = pl.multiple_of(j * 128, 128)
        other = t_ref[:, pl.ds(at, 128)].astype(F32)
        d_out[pl.ds(at, 128), :] = (x_ref[:, pl.ds(at, 128)].astype(F32) - other).T.astype(BF16)
        return carry

    lax.fori_loop(0, width // 128, turn_delta, 0)
    next(down_steps)

    here = {(0, 0)}

    def part(dl, dp, h):
        at = (dl % 8, dp)
        if at not in here:
            here.add(at)
            mail.wait(("tokens", -dl % 8, dp), cut(x_in, row_of(dl, dp), own_up), "y")
        return jnp.dot(
            turned[pl.ds(h * half_hid, half_hid), :],
            x_in[span(row_of(dl, dp), own_up), :],
            preferred_element_type=F32,
        )

    first = scatter_balanced(
        mail, "first", part, first_out, first_in, kept, "y", "xl", pre_ref
    )
    next(first)
    next(down_steps)
    next(first)
    next(down_steps)
    next(first)
    next(down_steps)
    next(first)
    next(down_steps)
    send_delta((0,))
    next(first)
    next(first)
    send_delta((1,))
    d_in[span(chip, 2 * own_down), :] = d_out[span(chip, 2 * own_down), :]

    pre = pre_ref[...].T * inv_width
    sig = jax.nn.sigmoid(pre)
    hid = (pre * sig).astype(BF16)
    slope = sig * (1.0 + pre * (1.0 - sig))
    for dl in range(8):
        for dp in range(2):
            mail.wait(("down sibling", dl, dp), down_slot(dl, dp, 1), "core")

    dh_ref[...] = jnp.zeros_like(dh_ref)

    def back(k, carry):
        at = pl.multiple_of(k * step, step)
        piece = down_all[pl.ds(at, step), :]
        mixed = lax.dot_general(hid, piece, NT, preferred_element_type=F32) * inv_hidden
        dy = (
            x_ref[:, pl.ds(at, step)].astype(F32) + mixed - t_ref[:, pl.ds(at, step)].astype(F32)
        ).astype(BF16)
        dh_ref[...] += jnp.dot(dy, piece, preferred_element_type=F32)
        return carry

    lax.fori_loop(0, steps, back, 0)
    dpre = dh_ref[...] * inv_hidden * slope
    dpre_all[row] = dpre.T.astype(BF16)

    def ordered(number, between):
        dl = picked(number, *between, [dl for dl, _ in ORDER])
        dp = picked(number, *between, [dp for _, dp in ORDER])
        return dl, dp

    acc_up[...] = jnp.zeros_like(acc_up)

    def up_path(between, number, carry):
        p = row_of(*ordered(number, between))
        grad = (
            lax.dot_general(
                x_in[span(p, own_up), :], dpre_all[p], NT, preferred_element_type=F32
            )
            * inv_width
        )
        acc_up[...] += packed_sum(grad, member_up[p, col].astype(F32) * path_rate[p, col])
        return carry

    for between, _ in zip(READY, gather_balanced(mail, "dpre", dpre_slot, "y", "xl")):
        if between:
            lax.fori_loop(*between, functools.partial(up_path, between), 0)
    count_up = lax.fori_loop(
        0, N_ROW, lambda p, count: count + member_up[p, col].astype(F32), jnp.float32(0.0)
    )
    loads[4].wait()
    loads[5].wait()
    average = acc_up[...] / count_up
    momentum = 0.9 * mu_ref[...] + average
    new_mu[...] = momentum
    fresh = wu_ref[...].astype(F32) - 0.7 * (average + 0.9 * momentum)
    new_up[...] = fresh.astype(BF16)
    turned[...] = fresh.T.astype(BF16)

    for _ in scatter_balanced(
        mail, "second", part, second_out, second_in, kept, "y", "xl", pre_ref
    ):
        pass
    pre_again = pre_ref[...] * inv_width
    hid_all[chip] = (pre_again * jax.nn.sigmoid(pre_again)).astype(BF16)

    acc_down[...] = jnp.zeros_like(acc_down)

    def down_path(between, number, carry):
        dl, dp = ordered(number, between)
        q = chip_of(dl, dp)
        acts = hid_all[q]
        mixed = (
            jnp.dot(
                down_all[span(chip, 2 * own_down), :], acts, preferred_element_type=F32
            )
            * inv_hidden
        )
        dy = (d_in[span(q, 2 * own_down), :].astype(F32) + mixed).astype(BF16)
        grad = lax.dot_general(dy, acts, NT, preferred_element_type=F32) * inv_hidden
        c = q * 2 + core
        acc_down[...] += packed_sum(grad, member_down[row, c].astype(F32) * path_rate[row, c])
        return carry

    for between, _ in zip(READY, gather_balanced(mail, "hid", hid_slot, "z", "xh")):
        if between:
            for dl, dp in ORDER[slice(*between)]:
                if dl or dp:
                    mail.wait(
                        ("delta", -dl % 8, dp), cut(d_in, chip_of(dl, dp), 2 * own_down), "z"
                    )
            lax.fori_loop(*between, functools.partial(down_path, between), 0)
    mail.send(("sums",), cut(acc_down, 1 - core, own_down), acc_sibling, core=1)
    count_down = lax.fori_loop(
        0, N_COL, lambda q, count: count + member_down[row, q].astype(F32), jnp.float32(0.0)
    )
    mail.wait(("sums",), acc_sibling, "core")
    average_down = (acc_down[span(core, own_down), :] + acc_sibling[...]) / count_down
    momentum_down = 0.9 * md_ref[...] + average_down
    new_md[...] = momentum_down
    own = down_all[span(col, own_down), :].astype(F32)
    new_down[...] = (own - 0.7 * (average_down + 0.9 * momentum_down)).astype(BF16)
    mail.finish()


def per_device(
    tokens, targets, w_up, w_down, up_momentum, down_momentum, member_up, member_down, path_rate
):
    rows, width = tokens.shape
    own_up, hidden = w_up.shape[1:]
    own_down = w_down.shape[1]
    vmem = pl.BlockSpec(memory_space=pltpu.VMEM)
    smem = pl.BlockSpec(memory_space=pltpu.SMEM)
    messages, sums = 200, 30
    outs = pl.pallas_call(
        kernel,
        out_shape=(
            jax.ShapeDtypeStruct((own_up, hidden), BF16),
            jax.ShapeDtypeStruct((own_up, hidden), F32),
            jax.ShapeDtypeStruct((own_down, hidden), BF16),
            jax.ShapeDtypeStruct((own_down, hidden), F32),
        ),
        in_specs=[pl.BlockSpec(memory_space=pl.ANY)] * 6 + [smem] * 3,
        out_specs=(vmem,) * 4,
        scratch_shapes=[
            pltpu.VMEM((rows, width), BF16),
            pltpu.VMEM((rows, width), BF16),
            pltpu.VMEM((own_up, hidden), BF16),
            pltpu.VMEM((own_up, hidden), F32),
            pltpu.VMEM((own_down, hidden), F32),
            pltpu.VMEM((hidden, own_up), BF16),
            pltpu.VMEM((width, hidden), BF16),
            pltpu.VMEM((width, rows), BF16),
            pltpu.VMEM((width, rows), BF16),
            pltpu.VMEM((width, rows), BF16),
            pltpu.VMEM((width, rows), BF16),
            pltpu.VMEM((N_ROW, hidden, rows), BF16),
            pltpu.VMEM((N_COL // 2, hidden, rows), BF16),
            pltpu.VMEM((rows, hidden), F32),
            pltpu.VMEM((hidden, rows), F32),
            pltpu.VMEM((4, hidden // 2, rows), F32),
            pltpu.VMEM((sums, hidden // 2, rows), BF16),
            pltpu.VMEM((sums, hidden // 2, rows), BF16),
            pltpu.VMEM((sums, hidden // 2, rows), BF16),
            pltpu.VMEM((sums, hidden // 2, rows), BF16),
            pltpu.VMEM((own_up, hidden), F32),
            pltpu.VMEM((2 * own_down, hidden), F32),
            pltpu.VMEM((own_down, hidden), F32),
            pltpu.SemaphoreType.DMA((messages,)),
            pltpu.SemaphoreType.DMA((messages,)),
            pltpu.SemaphoreType.DMA((6,)),
        ],
        compiler_params=pltpu.CompilerParams(
            collective_id=0, has_side_effects=True, vmem_limit_bytes=56 * 1024 * 1024
        ),
        name="path_mixture",
    )(
        tokens,
        targets,
        w_up[0],
        w_down[0],
        up_momentum[0],
        down_momentum[0],
        member_up,
        member_down,
        path_rate,
    )
    return tuple(out[None] for out in outs)


def solution(mesh):
    torus = Mesh(mesh.devices.reshape(tuple(AXES.values())), tuple(AXES))
    placed = (
        P(ROW + COL, None),
        P(ROW + COL, None),
        P(COL, ROW, None),
        P(ROW, COL, None),
        P(COL, ROW, None),
        P(ROW, COL, None),
        P(),
        P(),
        P(),
    )
    return jax.shard_map(
        per_device,
        mesh=torus,
        in_specs=placed,
        out_specs=(
            P(COL, ROW, None),
            P(COL, ROW, None),
            P(ROW, COL, None),
            P(ROW, COL, None),
        ),
        check_vma=False,
    )
```

time: 205 us -> 151 us (0.74)
  Pallas kernels: 200 us -> 145 us
    pallas_call x1, Pallas kernels: 200 us -> 145 us  [per_device(): pl.pallas_call(kernel, out_shape=(jax.ShapeDtypeStruct((own_up, hidden),...]
where the time goes in v2:
time: 151 us; the launch traced here: 150 us
  Pallas kernels  145 us (96%)
  local copies, waits for them, and re-layouts  4.36 us (3%)
    pallas_call x1, Pallas kernels, per_device(): pl.pallas_call(kernel, out_shape=(jax.ShapeDtypeStruct((own_up, hidden),...  145 us
    unnamed x10, local copies, waits for them, and re-layouts  4.36 us

profile of v2, /device:TPU:1, one launch (start us, length us, event | category | flops | bytes accessed | tf_op | source)
XLA Modules:
  0.0 150.4 jit_solution(17167292895292781957)
XLA Ops:
  0.6 145.4 %path_mixture.1 = (bf16[224,448]{1,0:T(8,128)(2,1)}, f32[224,448]{1,0:T(8,128)}, bf16[112,448]{1,0:T(8,128)(2,1)}, f32[112,448]{1,0:T(8,128)}) custom-call(bf16[128,3584]{1,0:T(8,128)(2,1)} %x_hbm.1, bf16[128,3584]{1,0:T(8,128)(2,1)} %t_hbm.1, bf16[224,448]{1,0:T(8,128)(2,1)} %bitcast.10, bf16[112,448]{1,0:T(8,128)(2,1)} %bitcast.15, f32[224,448]{1,0:T(8,128)} %bitcast.9, ...), custom_call_target="tpu_custom_call" | custom-call | tf_op jit(solution)/shard_map/path_mixture/pallas_call | solution.py:551
  146.0 0.0 copy-start
  146.0 1.7 %copy.17 = bf16[1,224,448]{2,1,0:T(8,128)(2,1)} copy(bf16[1,224,448]{2,1,0:T(8,128)(2,1)} %bitcast.13) | data formatting | bytes 401408
  147.7 0.0 copy-done
  147.7 0.0 copy-start.2
  147.7 0.8 copy.18
  148.5 0.2 copy-done.2
  148.7 0.0 copy-start.1
  148.7 0.6 copy.19
  149.4 0.3 copy-done.1
  149.7 0.7 copy.20
Async XLA Ops:
  146.0 1.7 %copy-start = (f32[224,448]{1,0:T(8,128)S(1)}, f32[224,448]{1,0:T(8,128)}, u32[]{:S(2)}) copy-start(f32[224,448]{1,0:T(8,128)} %get-tuple-element.9) | copy-start | bytes 1204228
  147.7 1.0 copy-start.2
  148.7 1.0 copy-start.1

commit v3 on v2

--- a/solution.py
+++ b/solution.py
@@ -44,14 +44,19 @@
         device = {axis: shifted(axis, step) for axis, step in steps.items()}
         copy = self.copy(key, (src, dst), device)
         copy.start()
-        self.sent.append(copy)
+        self.sent.append((key, copy))
 
     def wait(self, key, slot, axis):
         self.copy(key, (slot, slot), {axis: shifted(axis, 1)}).wait_recv()
 
-    def finish(self):
-        for copy in self.sent:
-            copy.wait_send()
+    def flush(self, name=None):
+        rest = []
+        for key, copy in self.sent:
+            if name in (None, key[0]):
+                copy.wait_send()
+            else:
+                rest.append((key, copy))
+        self.sent = rest
 
 
 def gather_balanced(mail, name, slot, line, pair):
@@ -137,8 +142,45 @@
     return found
 
 
-def scatter_balanced(mail, name, part, outgoing, incoming, kept, line, pair, result):
-    places = {}
+def gather_ring(mail, name, slot, line):
+    def send(way, d, h):
+        ref = slot(way * (1 - d), h)
+        mail.send((name, way, d, h), ref, ref, **{line: way})
+
+    ways = (1, -1)
+    for h in (0, 1):
+        for way in ways:
+            send(way, 1, h)
+    yield
+    for d in (1, 2, 3):
+        for h in (0, 1):
+            for way in ways:
+                mail.wait((name, way, d, h), slot(-d * way, h), line)
+                if d < 3 or way == 1 - 2 * h:
+                    send(way, d + 1, h)
+        yield
+    for h in (0, 1):
+        mail.wait((name, 1 - 2 * h, 4, h), slot(4, h), line)
+    yield
+
+
+RING_ORDER = (0, -1, 1, -2, 2, -3, 3, 4)
+RING_READY = (None, (0, 3), (3, 5), (5, 7), (7, 8))
+
+
+def scatter_balanced(
+    mail, name, prepare, terms, outgoing, incoming, line, pair, early, result
+):
+    places, made = {}, {}
+    half = result.shape[0] // 2
+
+    def ready(*offsets):
+        for dl, dp in offsets:
+            at = made.setdefault((dl % 8, dp), len(made))
+            terms[at] = prepare(dl, dp)
+
+    def term(dl, dp, h):
+        return terms[made[dl % 8, dp], pl.ds(h * half, half), :]
 
     def place(key):
         return places.setdefault(key, len(places))
@@ -153,50 +195,58 @@
         mail.wait((name, *key), incoming.at[at], axis)
         return incoming[at].astype(F32)
 
+    def send_near():
+        for h in (0, 1):
+            for way in ways:
+                send(("p", way, 1, h), term(way, 1, h), **{pair: 1})
+        for h in (0, 1):
+            send(("p", 0, 0, h), term(0, 1, h), **{pair: 1})
+
     ways = (1, -1)
-    for dp in (0, 1):
-        for h in (0, 1):
-            way = 1 - 2 * h
-            send(("l", way, 4, dp, h), part(4, dp, h), **{line: way})
-    yield
-    for h in (0, 1):
-        way = 2 * h - 1
-        for dp in (0, 1):
-            send(("l", way, 3, dp, h), part(3 * way, dp, h), **{line: way})
+    ready((4, 0), (4, 1))
     for h in (0, 1):
         way = 1 - 2 * h
         for dp in (1, 0):
-            total = part(3 * way, dp, h) + take(("l", way, 4, dp, h), line)
+            send(("l", way, 4, dp, h), term(4, dp, h), **{line: way})
+    yield
+    ready((3, 1), (3, 0), (-3, 1), (-3, 0))
+    for h in (0, 1):
+        way = 2 * h - 1
+        for dp in (1, 0):
+            send(("l", way, 3, dp, h), term(3 * way, dp, h), **{line: way})
+    if early:
+        ready((1, 1), (-1, 1), (0, 1))
+        send_near()
+    for h in (0, 1):
+        way = 1 - 2 * h
+        for dp in (1, 0):
+            total = term(3 * way, dp, h) + take(("l", way, 4, dp, h), line)
             send(("l", way, 3, dp, h), total, **{line: way})
     yield
+    ready((2, 1), (-2, 1), (2, 0), (-2, 0))
     for h in (0, 1):
         for way in (2 * h - 1, 1 - 2 * h):
-            total = part(2 * way, 1, h) + take(("l", way, 3, 1, h), line)
+            total = term(2 * way, 1, h) + take(("l", way, 3, 1, h), line)
             send(("p", way, 2, h), total, **{pair: 1})
+    yield
+    if not early:
+        ready((1, 1), (-1, 1), (0, 1))
+        send_near()
+    ready((1, 0), (-1, 0), (0, 0))
     for h in (0, 1):
         for way in (2 * h - 1, 1 - 2 * h):
-            total = part(2 * way, 0, h) + take(("l", way, 3, 0, h), line)
-            kept[2 * h + ways.index(way)] = total
-    for h in (0, 1):
-        for way in ways:
-            send(("p", way, 1, h), part(way, 1, h), **{pair: 1})
-    yield
-    for h in (0, 1):
-        for way in (2 * h - 1, 1 - 2 * h):
-            total = kept[2 * h + ways.index(way)] + take(("p", way, 2, h), pair)
+            total = term(2 * way, 0, h) + take(("l", way, 3, 0, h), line)
+            total = total + take(("p", way, 2, h), pair)
             send(("l", way, 2, h), total, **{line: way})
-    for h in (0, 1):
-        send(("p", 0, 0, h), part(0, 1, h), **{pair: 1})
-    yield
-    for h in (0, 1):
-        for way in ways:
-            total = part(way, 0, h) + take(("p", way, 1, h), pair)
+    yield
+    for h in (0, 1):
+        for way in ways:
+            total = term(way, 0, h) + take(("p", way, 1, h), pair)
             total = total + take(("l", way, 2, h), line)
             send(("l", way, 1, h), total, **{line: way})
     yield
-    half = result.shape[0] // 2
-    for h in (0, 1):
-        total = part(0, 0, h) + take(("p", 0, 0, h), pair)
+    for h in (0, 1):
+        total = term(0, 0, h) + take(("p", 0, 0, h), pair)
         for way in ways:
             total = total + take(("l", way, 1, h), line)
         result[pl.ds(h * half, half), :] = total
@@ -241,7 +291,10 @@
     spread = jnp.sqrt(jnp.mean(grad * grad, axis=-1, keepdims=True) + 1e-05)
     top = jnp.max(size, axis=-1, keepdims=True)
     largest = top / (top + spread) + 1e-06
-    quant = (grad / ((size + spread) * largest)).astype(BF16)
+    divisor = (size + spread) * largest
+    inverse = pl.reciprocal(divisor, approx=True)
+    inverse = inverse * (2.0 - divisor * inverse)
+    quant = (grad * inverse).astype(BF16)
     return quant.astype(F32) * (weight * largest)
 
 
@@ -251,20 +304,17 @@
     wu_hbm,
     wd_hbm,
     mu_hbm,
-    md_hbm,
     member_up,
     member_down,
     path_rate,
-    new_up,
-    new_mu,
-    new_down,
-    new_md,
+    mean_up,
+    mean_down,
     x_ref,
     t_ref,
     wu_ref,
     mu_ref,
-    md_ref,
     turned,
+    own_rows,
     down_all,
     x_out,
     x_in,
@@ -274,21 +324,23 @@
     hid_all,
     dh_ref,
     pre_ref,
-    kept,
+    terms,
     first_out,
     first_in,
     second_out,
     second_in,
     acc_up,
     acc_down,
-    acc_sibling,
+    sums_in,
+    pair_out,
+    pair_in,
     send_sems,
     recv_sems,
     local_sems,
 ):
     rows, width = x_ref.shape
     own_up, hidden = wu_ref.shape
-    own_down = md_ref.shape[0]
+    own_down = mean_down.shape[0]
     inv_width = width ** (-0.5)
     inv_hidden = hidden ** (-0.5)
     step = 512
@@ -300,18 +352,17 @@
     chip = xh * 8 + z
 
     peers = [(dl, dp) for dl in (4, 3, -3, 2, -2, 1, -1, 0) for dp in (1, 0) if dl or dp]
+    ring = (4, 3, -3, 2, -2, 1, -1)
     barrier = pltpu.get_barrier_semaphore()
-    for dl, dp in peers:
-        for line, pair in (("y", "xl"), ("z", "xh")):
-            pl.semaphore_signal(
-                barrier,
-                inc=1,
-                device_id={line: shifted(line, dl), pair: shifted(pair, dp)},
-                device_id_type=MESH,
-            )
-    pl.semaphore_signal(
-        barrier, inc=1, device_id={"core": shifted("core", 1)}, device_id_type=MESH
-    )
+    partners = [{"y": dl, "xl": dp} for dl, dp in peers]
+    partners += [{"z": dl} for dl in ring] + [{"xh": 1}, {"core": 1}]
+    for steps_to in partners:
+        pl.semaphore_signal(
+            barrier,
+            inc=1,
+            device_id={axis: shifted(axis, by) for axis, by in steps_to.items()},
+            device_id_type=MESH,
+        )
 
     def row_of(dl, dp):
         return lax.rem(y + (dl + 8), 8) * 2 + lax.rem(xl + dp, 2)
@@ -340,7 +391,6 @@
                 (wu_hbm, wu_ref),
                 (t_hbm, t_ref),
                 (mu_hbm, mu_ref),
-                (md_hbm, md_ref),
             )
         )
     ]
@@ -353,22 +403,36 @@
     def dpre_slot(dl, dp, h):
         return dpre_all.at[row_of(dl, dp), pl.ds(h * half_hid, half_hid)]
 
-    def hid_slot(dl, dp, h):
-        return hid_all.at[chip_of(dl, dp), pl.ds(h * half_hid, half_hid)]
+    def z_of(dl):
+        return lax.rem(z + (dl + 8), 8)
+
+    def hid_slot(dl, h):
+        return hid_all.at[z_of(dl), pl.ds(h * half_hid, half_hid)]
 
     def down_arrived(dl, dp):
         ref = down_slot(dl, dp)
         mail.send(("down sibling", dl % 8, dp), ref, ref, core=1)
 
-    def send_delta(pairs):
+    def send_delta(distances):
+        for dl in ring:
+            for v in (0, 1):
+                if abs(dl) in distances:
+                    mail.send(
+                        ("delta", dl % 8, v),
+                        cut(d_out, v * 8 + z_of(dl), 2 * own_down),
+                        cut(d_in, z * 2 + v, 2 * own_down),
+                        z=dl,
+                    )
+
+    def send_tokens(distances):
         for dl, dp in peers:
-            if dp in pairs:
+            if abs(dl) in distances:
                 mail.send(
-                    ("delta", dl % 8, dp),
-                    cut(d_out, chip_of(dl, dp), 2 * own_down),
-                    cut(d_in, chip, 2 * own_down),
-                    z=dl,
-                    xh=dp,
+                    ("tokens", dl % 8, dp),
+                    cut(x_out, row_of(dl, dp), own_up),
+                    cut(x_in, row, own_up),
+                    y=dl,
+                    xl=dp,
                 )
 
     loads[0].wait()
@@ -378,23 +442,18 @@
         x_out[pl.ds(at, 128), :] = x_ref[:, pl.ds(at, 128)].astype(F32).T.astype(BF16)
         return carry
 
-    lax.fori_loop(0, width // 128, turn, 0)
+    lax.fori_loop(0, width // 128, turn, 0, unroll=7)
     loads[1].wait()
-    pl.semaphore_wait(barrier, 2 * len(peers) + 1)
-    for dl, dp in peers:
-        mail.send(
-            ("tokens", dl % 8, dp),
-            cut(x_out, row_of(dl, dp), own_up),
-            cut(x_in, row, own_up),
-            y=dl,
-            xl=dp,
-        )
+    pl.semaphore_wait(barrier, len(partners))
+    send_tokens((4,))
     down_steps = gather_line(mail, "down", down_slot, "z", "xh", down_arrived)
-    next(down_steps)
 
     x_in[span(row, own_up), :] = x_out[span(row, own_up), :]
     loads[2].wait()
     turned[...] = wu_ref[...].astype(F32).T.astype(BF16)
+    mail.flush("tokens")
+    send_tokens((3,))
+    next(down_steps)
     loads[3].wait()
 
     def turn_delta(j, carry):
@@ -403,46 +462,49 @@
         d_out[pl.ds(at, 128), :] = (x_ref[:, pl.ds(at, 128)].astype(F32) - other).T.astype(BF16)
         return carry
 
-    lax.fori_loop(0, width // 128, turn_delta, 0)
-    next(down_steps)
+    lax.fori_loop(0, width // 128, turn_delta, 0, unroll=7)
 
     here = {(0, 0)}
 
-    def part(dl, dp, h):
+    def term(dl, dp):
         at = (dl % 8, dp)
         if at not in here:
             here.add(at)
             mail.wait(("tokens", -dl % 8, dp), cut(x_in, row_of(dl, dp), own_up), "y")
         return jnp.dot(
-            turned[pl.ds(h * half_hid, half_hid), :],
-            x_in[span(row_of(dl, dp), own_up), :],
-            preferred_element_type=F32,
+            turned[...], x_in[span(row_of(dl, dp), own_up), :], preferred_element_type=F32
         )
 
     first = scatter_balanced(
-        mail, "first", part, first_out, first_in, kept, "y", "xl", pre_ref
+        mail, "first", term, terms, first_out, first_in, "y", "xl", False, pre_ref
     )
+    next(first)
+    next(down_steps)
+    mail.flush("tokens")
+    send_tokens((2,))
+    next(first)
+    next(down_steps)
+    send_tokens((1, 0))
     next(first)
     next(down_steps)
     next(first)
     next(down_steps)
     next(first)
     next(down_steps)
+    send_delta((4, 3))
     next(first)
-    next(down_steps)
-    send_delta((0,))
-    next(first)
-    next(first)
-    send_delta((1,))
-    d_in[span(chip, 2 * own_down), :] = d_out[span(chip, 2 * own_down), :]
+    send_delta((2, 1))
+    for dl in range(8):
+        for dp in range(2):
+            mail.wait(("down sibling", dl, dp), down_slot(dl, dp, 1), "core")
+    for v in (0, 1):
+        d_in[span(z * 2 + v, 2 * own_down), :] = d_out[span(v * 8 + z, 2 * own_down), :]
+        own_rows[span(v, 2 * own_down), :] = down_all[span(v * 8 + z, 2 * own_down), :]
 
     pre = pre_ref[...].T * inv_width
     sig = jax.nn.sigmoid(pre)
     hid = (pre * sig).astype(BF16)
     slope = sig * (1.0 + pre * (1.0 - sig))
-    for dl in range(8):
-        for dp in range(2):
-            mail.wait(("down sibling", dl, dp), down_slot(dl, dp, 1), "core")
 
     dh_ref[...] = jnp.zeros_like(dh_ref)
 
@@ -456,7 +518,7 @@
         dh_ref[...] += jnp.dot(dy, piece, preferred_element_type=F32)
         return carry
 
-    lax.fori_loop(0, steps, back, 0)
+    lax.fori_loop(0, steps, back, 0, unroll=True)
     dpre = dh_ref[...] * inv_hidden * slope
     dpre_all[row] = dpre.T.astype(BF16)
 
@@ -480,63 +542,69 @@
 
     for between, _ in zip(READY, gather_balanced(mail, "dpre", dpre_slot, "y", "xl")):
         if between:
-            lax.fori_loop(*between, functools.partial(up_path, between), 0)
+            lax.fori_loop(*between, functools.partial(up_path, between), 0, unroll=True)
     count_up = lax.fori_loop(
         0, N_ROW, lambda p, count: count + member_up[p, col].astype(F32), jnp.float32(0.0)
     )
     loads[4].wait()
-    loads[5].wait()
     average = acc_up[...] / count_up
+    mean_up[...] = average
     momentum = 0.9 * mu_ref[...] + average
-    new_mu[...] = momentum
     fresh = wu_ref[...].astype(F32) - 0.7 * (average + 0.9 * momentum)
-    new_up[...] = fresh.astype(BF16)
     turned[...] = fresh.T.astype(BF16)
 
     for _ in scatter_balanced(
-        mail, "second", part, second_out, second_in, kept, "y", "xl", pre_ref
+        mail, "second", term, terms, second_out, second_in, "y", "xl", True, pre_ref
     ):
         pass
     pre_again = pre_ref[...] * inv_width
-    hid_all[chip] = (pre_again * jax.nn.sigmoid(pre_again)).astype(BF16)
+    hid_all[z] = (pre_again * jax.nn.sigmoid(pre_again)).astype(BF16)
 
     acc_down[...] = jnp.zeros_like(acc_down)
 
     def down_path(between, number, carry):
-        dl, dp = ordered(number, between)
-        q = chip_of(dl, dp)
+        q = z_of(picked(number, *between, RING_ORDER))
         acts = hid_all[q]
-        mixed = (
-            jnp.dot(
-                down_all[span(chip, 2 * own_down), :], acts, preferred_element_type=F32
-            )
-            * inv_hidden
+        mixed = jnp.dot(own_rows[...], acts, preferred_element_type=F32) * inv_hidden
+        dy = (d_in[span(q, 4 * own_down), :].astype(F32) + mixed).astype(BF16)
+        grad = lax.dot_general(dy, acts, NT, preferred_element_type=F32) * inv_hidden
+        c = xh * 16 + q * 2 + core
+        weight = member_down[row, c].astype(F32) * path_rate[row, c]
+        acc_down[...] += packed_sum(grad, weight)
+        return carry
+
+    for between, _ in zip(RING_READY, gather_ring(mail, "hid", hid_slot, "z")):
+        if between:
+            first_place, last_place = between
+            for dl in RING_ORDER[first_place:last_place]:
+                for v in (0, 1):
+                    if dl:
+                        mail.wait(
+                            ("delta", -dl % 8, v), cut(d_in, z_of(dl) * 2 + v, 2 * own_down), "z"
+                        )
+            lax.fori_loop(*between, functools.partial(down_path, between), 0, unroll=True)
+    for v in (0, 1):
+        mail.send(
+            ("sums", v),
+            cut(acc_down, v * 2 + 1 - core, own_down),
+            cut(sums_in, v, own_down),
+            core=1,
         )
-        dy = (d_in[span(q, 2 * own_down), :].astype(F32) + mixed).astype(BF16)
-        grad = lax.dot_general(dy, acts, NT, preferred_element_type=F32) * inv_hidden
-        c = q * 2 + core
-        acc_down[...] += packed_sum(grad, member_down[row, c].astype(F32) * path_rate[row, c])
-        return carry
-
-    for between, _ in zip(READY, gather_balanced(mail, "hid", hid_slot, "z", "xh")):
-        if between:
-            for dl, dp in ORDER[slice(*between)]:
-                if dl or dp:
-                    mail.wait(
-                        ("delta", -dl % 8, dp), cut(d_in, chip_of(dl, dp), 2 * own_down), "z"
-                    )
-            lax.fori_loop(*between, functools.partial(down_path, between), 0)
-    mail.send(("sums",), cut(acc_down, 1 - core, own_down), acc_sibling, core=1)
     count_down = lax.fori_loop(
         0, N_COL, lambda q, count: count + member_down[row, q].astype(F32), jnp.float32(0.0)
     )
-    mail.wait(("sums",), acc_sibling, "core")
-    average_down = (acc_down[span(core, own_down), :] + acc_sibling[...]) / count_down
-    momentum_down = 0.9 * md_ref[...] + average_down
-    new_md[...] = momentum_down
-    own = down_all[span(col, own_down), :].astype(F32)
-    new_down[...] = (own - 0.7 * (average_down + 0.9 * momentum_down)).astype(BF16)
-    mail.finish()
+    for v in (0, 1):
+        mail.wait(("sums", v), cut(sums_in, v, own_down), "core")
+
+    def both_cores(v):
+        return acc_down[span(v * 2 + core, own_down), :] + sums_in[span(v, own_down), :]
+
+    pair_out[...] = both_cores(1 - xh).astype(BF16)
+    mail.send(("pair",), pair_out, pair_in, xh=1)
+    own_sums = both_cores(xh)
+    mail.wait(("pair",), pair_in, "xh")
+    mean_down[...] = (own_sums + pair_in[...].astype(F32)) / count_down
+    mail.flush()
 
 
 def per_device(
@@ -548,43 +616,43 @@
     vmem = pl.BlockSpec(memory_space=pltpu.VMEM)
     smem = pl.BlockSpec(memory_space=pltpu.SMEM)
     messages, sums = 200, 30
-    outs = pl.pallas_call(
+    means = pl.pallas_call(
         kernel,
         out_shape=(
-            jax.ShapeDtypeStruct((own_up, hidden), BF16),
             jax.ShapeDtypeStruct((own_up, hidden), F32),
-            jax.ShapeDtypeStruct((own_down, hidden), BF16),
             jax.ShapeDtypeStruct((own_down, hidden), F32),
         ),
-        in_specs=[pl.BlockSpec(memory_space=pl.ANY)] * 6 + [smem] * 3,
-        out_specs=(vmem,) * 4,
+        in_specs=[pl.BlockSpec(memory_space=pl.ANY)] * 5 + [smem] * 3,
+        out_specs=(vmem,) * 2,
         scratch_shapes=[
             pltpu.VMEM((rows, width), BF16),
             pltpu.VMEM((rows, width), BF16),
             pltpu.VMEM((own_up, hidden), BF16),
             pltpu.VMEM((own_up, hidden), F32),
-            pltpu.VMEM((own_down, hidden), F32),
             pltpu.VMEM((hidden, own_up), BF16),
+            pltpu.VMEM((4 * own_down, hidden), BF16),
             pltpu.VMEM((width, hidden), BF16),
             pltpu.VMEM((width, rows), BF16),
             pltpu.VMEM((width, rows), BF16),
             pltpu.VMEM((width, rows), BF16),
             pltpu.VMEM((width, rows), BF16),
             pltpu.VMEM((N_ROW, hidden, rows), BF16),
-            pltpu.VMEM((N_COL // 2, hidden, rows), BF16),
+            pltpu.VMEM((AXES["z"], hidden, rows), BF16),
             pltpu.VMEM((rows, hidden), F32),
             pltpu.VMEM((hidden, rows), F32),
-            pltpu.VMEM((4, hidden // 2, rows), F32),
+            pltpu.VMEM((N_ROW, hidden, rows), F32),
             pltpu.VMEM((sums, hidden // 2, rows), BF16),
             pltpu.VMEM((sums, hidden // 2, rows), BF16),
             pltpu.VMEM((sums, hidden // 2, rows), BF16),
             pltpu.VMEM((sums, hidden // 2, rows), BF16),
             pltpu.VMEM((own_up, hidden), F32),
+            pltpu.VMEM((4 * own_down, hidden), F32),
             pltpu.VMEM((2 * own_down, hidden), F32),
-            pltpu.VMEM((own_down, hidden), F32),
+            pltpu.VMEM((own_down, hidden), BF16),
+            pltpu.VMEM((own_down, hidden), BF16),
             pltpu.SemaphoreType.DMA((messages,)),
             pltpu.SemaphoreType.DMA((messages,)),
-            pltpu.SemaphoreType.DMA((6,)),
+            pltpu.SemaphoreType.DMA((5,)),
         ],
         compiler_params=pltpu.CompilerParams(
             collective_id=0, has_side_effects=True, vmem_limit_bytes=56 * 1024 * 1024
@@ -596,12 +664,16 @@
         w_up[0],
         w_down[0],
         up_momentum[0],
-        down_momentum[0],
         member_up,
         member_down,
         path_rate,
     )
-    return tuple(out[None] for out in outs)
+    outs = []
+    for matrix, old, mean in ((w_up, up_momentum, means[0]), (w_down, down_momentum, means[1])):
+        momentum = 0.9 * old + mean[None]
+        fresh = matrix.astype(F32) - 0.7 * (mean[None] + 0.9 * momentum)
+        outs += [fresh.astype(BF16), momentum]
+    return tuple(outs)
 
 
 def solution(mesh):

time: 151 us -> 138 us (0.914)
  Pallas kernels: 145 us -> 133 us
  local copies, waits for them, and re-layouts: 4.36 us -> 0.03 us
  other arithmetic: 0 us -> 2.83 us
    pallas_call x1, Pallas kernels: 145 us -> 133 us  [per_device(): pl.pallas_call(kernel, out_shape=(jax.ShapeDtypeStruct((own_up, hidden),...]
    unnamed x10, local copies, waits for them, and re-layouts: 4.36 us -> 0.03 us
    convert_element_type x0 -> x2, other arithmetic: none -> 2.83 us  [per_device(): outs += [fresh.astype(BF16), momentum]]
where the time goes in v3:
time: 138 us; the launch traced here: 137 us
  Pallas kernels  133 us (96%)
  other arithmetic  2.83 us (2%)
    pallas_call x1, Pallas kernels, per_device(): pl.pallas_call(kernel, out_shape=(jax.ShapeDtypeStruct((own_up, hidden),...  133 us
    convert_element_type x2, other arithmetic, per_device(): outs += [fresh.astype(BF16), momentum]  2.83 us

profile of v3, /device:TPU:1, one launch (start us, length us, event | category | flops | bytes accessed | tf_op | source)
XLA Modules:
  0.0 137.0 jit_solution(7157604836128066938)
XLA Ops:
  0.6 0.0 copy-start
  0.6 0.0 copy-start.1
  0.7 133.4 %path_mixture.1 = (f32[224,448]{1,0:T(8,128)}, f32[112,448]{1,0:T(8,128)}) custom-call(bf16[128,3584]{1,0:T(8,128)(2,1)} %x_hbm.1, bf16[128,3584]{1,0:T(8,128)(2,1)} %t_hbm.1, bf16[224,448]{1,0:T(8,128)(2,1)} %bitcast.24, bf16[112,448]{1,0:T(8,128)(2,1)} %bitcast.25, f32[224,448]{1,0:T(8,128)} %bitcast.23, s32[16,32]{1,0:T(8,128)} %member_up.1, ...), custom_call_target="tpu_custom_call" | custom-call | tf_op jit(solution)/shard_map/path_mixture/pallas_call | solution.py:619
  134.1 0.0 copy-done
  134.1 0.0 copy-done.1
  134.1 0.0 copy-start.2
  134.1 0.0 copy-start.3
  134.1 0.0 copy-start.4
  134.1 2.0 %fusion.2 = (bf16[1,224,448]{2,1,0:T(8,128)(2,1)}, f32[1,224,448]{2,1,0:T(8,128)}) fusion(f32[224,448]{1,0:T(8,128)} %get-tuple-element.6, bf16[1,224,448]{2,1,0:T(8,128)(2,1)S(1)} %copy-done.1, f32[1,224,448]{2,1,0:T(8,128)S(1)} %copy-done), kind=kLoop, calls=%fused_computation.4 | loop fusion | flops 802816 | bytes 1605632 | tf_op jit(solution)/shard_map/convert_element_type | solution.py:675
  136.2 0.0 copy-done.2
  136.2 0.0 copy-done.3
  136.2 0.0 copy-done.4
  136.2 0.8 fusion.5
Async XLA Ops:
  0.6 133.4 %copy-start = (f32[1,224,448]{2,1,0:T(8,128)S(1)}, f32[1,224,448]{2,1,0:T(8,128)}, u32[]{:S(2)}) copy-start(f32[1,224,448]{2,1,0:T(8,128)} %param.13) | copy-start | bytes 1204228
  0.6 133.4 %copy-start.1 = (bf16[1,224,448]{2,1,0:T(8,128)(2,1)S(1)}, bf16[1,224,448]{2,1,0:T(8,128)(2,1)}, u32[]{:S(2)}) copy-start(bf16[1,224,448]{2,1,0:T(8,128)(2,1)} %param.11) | copy-start | bytes 602116
  134.1 2.1 %copy-start.2 = (bf16[1,112,448]{2,1,0:T(8,128)(2,1)S(1)}, bf16[1,112,448]{2,1,0:T(8,128)(2,1)}, u32[]{:S(2)}) copy-start(bf16[1,112,448]{2,1,0:T(8,128)(2,1)} %param.12) | copy-start | bytes 301060
  134.1 2.1 %copy-start.3 = (f32[1,112,448]{2,1,0:T(8,128)S(1)}, f32[1,112,448]{2,1,0:T(8,128)}, u32[]{:S(2)}) copy-start(f32[1,112,448]{2,1,0:T(8,128)} %param.14) | copy-start | bytes 602116
  134.1 2.1 %copy-start.4 = (f32[112,448]{1,0:T(8,128)S(1)}, f32[112,448]{1,0:T(8,128)}, u32[]{:S(2)}) copy-start(f32[112,448]{1,0:T(8,128)} %get-tuple-element.7) | copy-start | bytes 602116

commit v4 on v3

--- a/solution.py
+++ b/solution.py
@@ -142,30 +142,32 @@
     return found
 
 
-def gather_ring(mail, name, slot, line):
+def gather_ring(mail, name, slot, line, pieces):
     def send(way, d, h):
         ref = slot(way * (1 - d), h)
         mail.send((name, way, d, h), ref, ref, **{line: way})
 
     ways = (1, -1)
-    for h in (0, 1):
+    last_way = [1 if 2 * h < pieces else -1 for h in range(pieces)]
+    for h in range(pieces):
         for way in ways:
             send(way, 1, h)
-    yield
+        if 2 * (h + 1) in (pieces, 2 * pieces):
+            yield
     for d in (1, 2, 3):
-        for h in (0, 1):
+        for h in range(pieces):
             for way in ways:
                 mail.wait((name, way, d, h), slot(-d * way, h), line)
-                if d < 3 or way == 1 - 2 * h:
+                if d < 3 or way == last_way[h]:
                     send(way, d + 1, h)
         yield
-    for h in (0, 1):
-        mail.wait((name, 1 - 2 * h, 4, h), slot(4, h), line)
+    for h in range(pieces):
+        mail.wait((name, last_way[h], 4, h), slot(4, h), line)
     yield
 
 
 RING_ORDER = (0, -1, 1, -2, 2, -3, 3, 4)
-RING_READY = (None, (0, 3), (3, 5), (5, 7), (7, 8))
+RING_READY = ((0, 3), (3, 5), (5, 7), (7, 8))
 
 
 def scatter_balanced(
@@ -250,7 +252,7 @@
         for way in ways:
             total = total + take(("l", way, 1, h), line)
         result[pl.ds(h * half, half), :] = total
-    yield
+        yield
 
 
 def gather_line(mail, name, slot, line, pair, arrived):
@@ -381,6 +383,7 @@
 
     mail = Mail(send_sems, recv_sems)
     half_hid = hidden // 2
+    pieces = 2
 
     loads = [
         pltpu.make_async_copy(src, dst, local_sems.at[number])
@@ -407,7 +410,8 @@
         return lax.rem(z + (dl + 8), 8)
 
     def hid_slot(dl, h):
-        return hid_all.at[z_of(dl), pl.ds(h * half_hid, half_hid)]
+        size = hidden // pieces
+        return hid_all.at[z_of(dl), pl.ds(h * size, size)]
 
     def down_arrived(dl, dp):
         ref = down_slot(dl, dp)
@@ -451,7 +455,7 @@
     x_in[span(row, own_up), :] = x_out[span(row, own_up), :]
     loads[2].wait()
     turned[...] = wu_ref[...].astype(F32).T.astype(BF16)
-    mail.flush("tokens")
+
     send_tokens((3,))
     next(down_steps)
     loads[3].wait()
@@ -480,7 +484,7 @@
     )
     next(first)
     next(down_steps)
-    mail.flush("tokens")
+
     send_tokens((2,))
     next(first)
     next(down_steps)
@@ -491,9 +495,8 @@
     next(down_steps)
     next(first)
     next(down_steps)
-    send_delta((4, 3))
     next(first)
-    send_delta((2, 1))
+    next(first)
     for dl in range(8):
         for dp in range(2):
             mail.wait(("down sibling", dl, dp), down_slot(dl, dp, 1), "core")
@@ -543,6 +546,7 @@
     for between, _ in zip(READY, gather_balanced(mail, "dpre", dpre_slot, "y", "xl")):
         if between:
             lax.fori_loop(*between, functools.partial(up_path, between), 0, unroll=True)
+    send_delta((4, 3, 2, 1))
     count_up = lax.fori_loop(
         0, N_ROW, lambda p, count: count + member_up[p, col].astype(F32), jnp.float32(0.0)
     )
@@ -553,12 +557,16 @@
     fresh = wu_ref[...].astype(F32) - 0.7 * (average + 0.9 * momentum)
     turned[...] = fresh.T.astype(BF16)
 
-    for _ in scatter_balanced(
+    hid_steps = gather_ring(mail, "hid", hid_slot, "z", pieces)
+    second = scatter_balanced(
         mail, "second", term, terms, second_out, second_in, "y", "xl", True, pre_ref
-    ):
-        pass
-    pre_again = pre_ref[...] * inv_width
-    hid_all[z] = (pre_again * jax.nn.sigmoid(pre_again)).astype(BF16)
+    )
+    for stage, _ in enumerate(second):
+        if stage >= 5:
+            at = pl.ds((stage - 5) * half_hid, half_hid)
+            pre_again = pre_ref[at, :] * inv_width
+            hid_all[z, at, :] = (pre_again * jax.nn.sigmoid(pre_again)).astype(BF16)
+            next(hid_steps)
 
     acc_down[...] = jnp.zeros_like(acc_down)
 
@@ -573,7 +581,7 @@
         acc_down[...] += packed_sum(grad, weight)
         return carry
 
-    for between, _ in zip(RING_READY, gather_ring(mail, "hid", hid_slot, "z")):
+    for between, _ in zip(RING_READY, hid_steps):
         if between:
             first_place, last_place = between
             for dl in RING_ORDER[first_place:last_place]:
@@ -615,7 +623,7 @@
     own_down = w_down.shape[1]
     vmem = pl.BlockSpec(memory_space=pltpu.VMEM)
     smem = pl.BlockSpec(memory_space=pltpu.SMEM)
-    messages, sums = 200, 30
+    messages, sums = 240, 30
     means = pl.pallas_call(
         kernel,
         out_shape=(

time: 138 us -> 132 us (0.957)
  Pallas kernels: 133 us -> 128 us
    pallas_call x1, Pallas kernels: 133 us -> 128 us  [per_device(): pl.pallas_call(kernel, out_shape=(jax.ShapeDtypeStruct((own_up, hidden),...]
where the time goes in v4:
time: 132 us
  Pallas kernels  128 us (97%)
  other arithmetic  2.83 us (2%)
    pallas_call x1, Pallas kernels, per_device(): pl.pallas_call(kernel, out_shape=(jax.ShapeDtypeStruct((own_up, hidden),...  128 us
    convert_element_type x2, other arithmetic, per_device(): outs += [fresh.astype(BF16), momentum]  2.83 us

profile of v4, /device:TPU:1, one launch (start us, length us, event | category | flops | bytes accessed | tf_op | source)
XLA Modules:
  0.0 131.7 jit_solution(1918199674524986097)
XLA Ops:
  0.6 0.0 copy-start
  0.6 0.0 copy-start.1
  0.7 128.2 %path_mixture.1 = (f32[224,448]{1,0:T(8,128)}, f32[112,448]{1,0:T(8,128)}) custom-call(bf16[128,3584]{1,0:T(8,128)(2,1)} %x_hbm.1, bf16[128,3584]{1,0:T(8,128)(2,1)} %t_hbm.1, bf16[224,448]{1,0:T(8,128)(2,1)} %bitcast.24, bf16[112,448]{1,0:T(8,128)(2,1)} %bitcast.25, f32[224,448]{1,0:T(8,128)} %bitcast.23, s32[16,32]{1,0:T(8,128)} %member_up.1, ...), custom_call_target="tpu_custom_call" | custom-call | tf_op jit(solution)/shard_map/path_mixture/pallas_call | solution.py:627
  128.8 0.0 copy-done
  128.9 0.0 copy-done.1
  128.9 0.0 copy-start.2
  128.9 0.0 copy-start.3
  128.9 0.0 copy-start.4
  128.9 2.0 %fusion.2 = (bf16[1,224,448]{2,1,0:T(8,128)(2,1)}, f32[1,224,448]{2,1,0:T(8,128)}) fusion(f32[224,448]{1,0:T(8,128)} %get-tuple-element.6, bf16[1,224,448]{2,1,0:T(8,128)(2,1)S(1)} %copy-done.1, f32[1,224,448]{2,1,0:T(8,128)S(1)} %copy-done), kind=kLoop, calls=%fused_computation.4 | loop fusion | flops 802816 | bytes 1605632 | tf_op jit(solution)/shard_map/convert_element_type | solution.py:683
  130.9 0.0 copy-done.2
  131.0 0.0 copy-done.3
  131.0 0.0 copy-done.4
  131.0 0.8 fusion.5
Async XLA Ops:
  0.6 128.2 %copy-start = (f32[1,224,448]{2,1,0:T(8,128)S(1)}, f32[1,224,448]{2,1,0:T(8,128)}, u32[]{:S(2)}) copy-start(f32[1,224,448]{2,1,0:T(8,128)} %param.13) | copy-start | bytes 1204228
  0.6 128.2 %copy-start.1 = (bf16[1,224,448]{2,1,0:T(8,128)(2,1)S(1)}, bf16[1,224,448]{2,1,0:T(8,128)(2,1)}, u32[]{:S(2)}) copy-start(bf16[1,224,448]{2,1,0:T(8,128)(2,1)} %param.11) | copy-start | bytes 602116
  128.9 2.1 %copy-start.2 = (bf16[1,112,448]{2,1,0:T(8,128)(2,1)S(1)}, bf16[1,112,448]{2,1,0:T(8,128)(2,1)}, u32[]{:S(2)}) copy-start(bf16[1,112,448]{2,1,0:T(8,128)(2,1)} %param.12) | copy-start | bytes 301060
  128.9 2.1 %copy-start.3 = (f32[1,112,448]{2,1,0:T(8,128)S(1)}, f32[1,112,448]{2,1,0:T(8,128)}, u32[]{:S(2)}) copy-start(f32[1,112,448]{2,1,0:T(8,128)} %param.14) | copy-start | bytes 602116
  128.9 2.1 %copy-start.4 = (f32[112,448]{1,0:T(8,128)S(1)}, f32[112,448]{1,0:T(8,128)}, u32[]{:S(2)}) copy-start(f32[112,448]{1,0:T(8,128)} %get-tuple-element.7) | copy-start | bytes 602116
